TPU v7x, 256 devices: a whole 4x4x8 slice. The times are simulated.
256 devices in a mesh: ctx: 32 (over z, x_lo, core), head: 8 (over x_hi, y).
Axes of the slice: x: 4 (x_hi: 2, x_lo: 2; x = x_hi * 2 + x_lo), y: 4, z: 8, core: 2. Of those that a mesh axis runs over, the one named last changes fastest.
Arguments:
- queries: bfloat16 [8192, 6144], P(('ctx', 'head')), may hold values from -113 to 113
- keys: bfloat16 [8192, 1024], P(('ctx', 'head')), may hold values from -4.6 to 4.6
- values: bfloat16 [8192, 1024], P(('ctx', 'head')), may hold values from -6 to 6
- fold_map: int32 [64], replicated, may hold values from 0 to 63, each once
- noisy: int32 [64], replicated, may hold values from 0 to 1, as said below
- noise_step: int32 [64], replicated, may hold values from 0 to 63
- gate_table: float32 [64, 6144], P(None, 'head'), may hold values from -1.5 to 1.5
Outputs:
- gated_update: bfloat16 [8192, 6144], P(('ctx', 'head'))
Inputs may be any that keep to these rules, and one draw needn't show every extreme that they name: `fold_map`: each position in span order appears once. The noisy spans are a trailing run of the span order holding between 16 and 48 spans.
All inputs are finite; a program needn't handle non-finite values.
Results may differ from a plain program's by a relative error of at most 0.006.
Values may be sent and summed in bfloat16 or wider, within the bound.
A program may use at most 64 MiB of HBM per device.

v0:
```python
import math

import jax
import jax.numpy as jnp
from jax import lax
from jax.sharding import PartitionSpec as P

HEADS = 48
KVH = 8
HD = 128
SPAN = 128


def span_order(fold_map, span_ids, start, width):
    positions = (start + jnp.arange(width, dtype=jnp.int32)) // SPAN
    match = (positions[:, None] == span_ids[None, :]).astype(jnp.int32)
    return jnp.sum(match * fold_map[None, :], axis=1)


def local(queries, keys, values, fold_map, noisy, noise_step, gate_table):
    query_here, keys_here, values_here = (
        lax.all_to_all(queries, "head", split_axis=1, concat_axis=0, tiled=True),
        lax.all_to_all(keys, "head", split_axis=1, concat_axis=0, tiled=True),
        lax.all_to_all(values, "head", split_axis=1, concat_axis=0, tiled=True),
    )
    tok_rows = query_here.shape[0]
    groups = keys_here.shape[1] // HD
    ratio = HEADS // KVH
    local_spans = tok_rows // SPAN
    total_spans = fold_map.shape[0]
    span_ids = jnp.arange(total_spans, dtype=jnp.int32)
    first_span = lax.axis_index("ctx") * local_spans
    my_order = lax.dynamic_slice_in_dim(fold_map, first_span, local_spans)
    picks = (my_order[:, None] == span_ids[None, :]).astype(jnp.int32)
    my_noisy = jnp.sum(picks * noisy[None, :], axis=1)
    my_step = jnp.sum(picks * noise_step[None, :], axis=1)
    query_order = jnp.repeat(my_order, SPAN)
    grouped = query_here.reshape(tok_rows, groups, ratio, HD)
    scale = HD ** (-0.5)

    def attend(carry, key_block, value_block, key_order):
        maxima, totals, accum = carry
        width = key_block.shape[0]
        scores = (
            jnp.einsum(
                "tgrd,pgd->grtp",
                grouped,
                key_block.reshape(width, groups, HD),
                preferred_element_type=jnp.float32,
            )
            * scale
        )
        seen = key_order[None, :] <= query_order[:, None]
        scores = jnp.where(seen[None, None], scores, -jnp.inf)
        newmax = jnp.maximum(maxima, jnp.max(scores, axis=-1))
        factor = jnp.exp(maxima - newmax)
        probs = jnp.exp(scores - newmax[..., None])
        totals = totals * factor + jnp.sum(probs, axis=-1)
        update = jnp.einsum(
            "grtp,pgd->tgrd",
            probs.astype(jnp.bfloat16),
            value_block.reshape(width, groups, HD),
            preferred_element_type=jnp.float32,
        )
        accum = accum * jnp.transpose(factor, (2, 0, 1))[..., None] + update
        return (newmax, totals, accum)

    start_max = jnp.full((groups, ratio, tok_rows), -1e30, jnp.float32)
    start_total = jnp.zeros((groups, ratio, tok_rows), jnp.float32)
    start_accum = jnp.zeros((tok_rows, groups, ratio, HD), jnp.float32)
    key_piece = lax.all_gather(keys_here, "ctx", axis=0, tiled=True)
    value_piece = lax.all_gather(values_here, "ctx", axis=0, tiled=True)
    length = key_piece.shape[0]
    shards = length // tok_rows
    block = math.gcd(shards, max(1, 512 // tok_rows)) * tok_rows
    count = length // block

    def one_block(block_number, state):
        offset = block_number * block
        key_block = lax.dynamic_slice_in_dim(key_piece, offset, block)
        value_block = lax.dynamic_slice_in_dim(value_piece, offset, block)
        key_order = span_order(fold_map, span_ids, offset, block)
        return attend(state, key_block, value_block, key_order)

    maxima, totals, accum = lax.fori_loop(
        0, count, one_block, (start_max, start_total, start_accum)
    )
    safe_totals = jnp.where(totals > 0.0, totals, jnp.float32(1.0))
    attended = accum / jnp.transpose(safe_totals, (2, 0, 1))[..., None]
    step_hot = (
        my_step[:, None] == jnp.arange(gate_table.shape[0], dtype=jnp.int32)[None, :]
    ).astype(jnp.float32)
    gate_rows = jnp.dot(step_hot, gate_table, precision=lax.Precision.HIGHEST)
    features = groups * ratio * HD
    mixed = attended.reshape(local_spans, SPAN, features) * gate_rows[:, None, :]
    mixed = jnp.where((my_noisy == 1)[:, None, None], mixed, jnp.float32(0.0))
    result = mixed.reshape(tok_rows, features).astype(jnp.bfloat16)
    return lax.all_to_all(result, "head", split_axis=0, concat_axis=1, tiled=True)


def solution(mesh):
    placed = (
        P(("ctx", "head"), None),
        P(("ctx", "head"), None),
        P(("ctx", "head"), None),
        P(),
        P(),
        P(),
        P(None, "head"),
    )
    return jax.shard_map(
        local, mesh=mesh, in_specs=placed, out_specs=P(("ctx", "head"), None), check_vma=False
    )
```

profile of v0, /device:TPU:1, one launch (start us, length us, event | category | flops | bytes accessed | tf_op | source)
XLA Modules:
  0.0 270.2 jit_solution(11054738207137543895)
XLA Ops:
  7.4 14.1 %all_to_all.70 = bf16[32,8,128]{2,0,1:T(8,128)(2,1)} all-to-all(bf16[32,8,128]{2,0,1:T(8,128)(2,1)S(1)} %copy_bitcast_fusion.2), channel_id=1, replica_groups=mesh['ctx'=32,'head'=8] {'head'}, dimensions={1} | all-to-all | bytes 131072 | tf_op jit(solution)/shard_map/all_to_all | solution.py:23
  22.5 9.8 %all_to_all.71 = bf16[32,8,128]{2,0,1:T(8,128)(2,1)} all-to-all(bf16[32,8,128]{2,0,1:T(8,128)(2,1)S(1)} %copy_bitcast_fusion.1), channel_id=1, replica_groups=mesh['ctx'=32,'head'=8] {'head'}, dimensions={1} | all-to-all | bytes 131072 | tf_op jit(solution)/shard_map/all_to_all | solution.py:24
  32.2 1.8 copy.51
  34.0 3.5 %all-to-all-start.1 = ((bf16[32,8,768]{2,0,1:T(8,128)(2,1)}), bf16[32,8,768]{2,0,1:T(8,128)(2,1)S(1)}, u32[]{:S(2)}, u32[]{:S(2)}) async-start(bf16[32,8,768]{2,0,1:T(8,128)(2,1)} %bitcast.86), calls=%async_computation.1 | async-start | bytes 786432 | tf_op jit(solution)/shard_map/all_to_all | solution.py:22
  39.6 6.4 %all-to-all-done.1 = bf16[32,8,768]{2,0,1:T(8,128)(2,1)S(1)} async-done(((bf16[32,8,768]{2,0,1:T(8,128)(2,1)}), bf16[32,8,768]{2,0,1:T(8,128)(2,1)S(1)}, u32[]{:S(2)}, u32[]{:S(2)}) %all-to-all-start.1) | async-done | bytes 393248 | tf_op jit(solution)/shard_map/all_to_all | solution.py:22
  47.2 39.6 %all-gather.3.cloned.1.call-done = bf16[8192,128]{1,0:T(8,128)(2,1)} async-done(((bf16[256,128]{1,0:T(8,128)(2,1)}), bf16[8192,128]{1,0:T(8,128)(2,1)}) %all-gather.3.cloned.1.call-update) | async-done | bytes 2097168 | tf_op jit(solution)/shard_map/all_gather | solution.py:71
  86.9 66.3 %all-gather.5.cloned.1.call-done = bf16[8192,128]{1,0:T(8,128)(2,1)} async-done(((bf16[256,128]{1,0:T(8,128)(2,1)}), bf16[8192,128]{1,0:T(8,128)(2,1)}) %all-gather.5.cloned.1.call-update) | async-done | bytes 2097168 | tf_op jit(solution)/shard_map/all_gather | solution.py:72
  153.1 92.1 %while.20 = (s32[]{:T(128)}, f32[1,6,256]{2,1,0:T(8,128)S(1)}, f32[1,6,256]{2,1,0:T(8,128)S(1)}, f32[256,1,6,128]{0,3,2,1:T(8,128)}, s32[64]{0:T(128)S(1)}, /*in...) while((s32[]{:T(128)}, f32[1,6,256]{2,1,0:T(8,128)S(1)}, ...), condition=%wide.region_5.6_spmd.clone, body=%wide.region_1.5_spmd.clone.sunk | while | flops 412140032 | bytes 12298699 | solution.py:85
  153.5 1.7 fusion.50
  155.2 2.7 %fusion.53 = f32[256,1,6,128]{0,3,2,1:T(8,128)} fusion(f32[512,256,6]{1,0,2:T(8,128)S(1)} %get-tuple-element.407, f32[6,256]{1,0:T(8,128)S(1)} %bitcast.111, pred[256,512]{0,1:T(8,128)(4,1)S(1)} %broadcast_compare_fusion.3, f32[256,1,6,128]{0,3,2,1:T(8,128)} %get-tuple-element.425, f32[256,6]{0,1:T(8,128)S(1)} %get-tuple-element.408, ...), kind=kOutput, calls=%fused_computation.14.clone.1 | convolution fusion | flops 205062144 | bytes 4993029 | tf_op jit(solution)/shard_map/while/body/eval_jaxpr/grtp,pgd->tgrd/dot_general | solution.py:59
  160.6 3.0 %fusion.53 = f32[256,1,6,128]{0,3,2,1:T(8,128)} fusion(f32[512,256,6]{1,0,2:T(8,128)S(1)} %get-tuple-element.407, f32[6,256]{1,0:T(8,128)S(1)} %bitcast.111, pred[256,512]{0,1:T(8,128)(4,1)S(1)} %broadcast_compare_fusion.3, f32[256,1,6,128]{0,3,2,1:T(8,128)} %get-tuple-element.425, f32[256,6]{0,1:T(8,128)S(1)} %get-tuple-element.408, ...), kind=kOutput, calls=%fused_computation.14.clone.1 | convolution fusion | flops 205062144 | bytes 4993029 | tf_op jit(solution)/shard_map/while/body/eval_jaxpr/grtp,pgd->tgrd/dot_general | solution.py:59
  164.7 1.7 fusion.50
  166.4 3.0 %fusion.53 = f32[256,1,6,128]{0,3,2,1:T(8,128)} fusion(f32[512,256,6]{1,0,2:T(8,128)S(1)} %get-tuple-element.407, f32[6,256]{1,0:T(8,128)S(1)} %bitcast.111, pred[256,512]{0,1:T(8,128)(4,1)S(1)} %broadcast_compare_fusion.3, f32[256,1,6,128]{0,3,2,1:T(8,128)} %get-tuple-element.425, f32[256,6]{0,1:T(8,128)S(1)} %get-tuple-element.408, ...), kind=kOutput, calls=%fused_computation.14.clone.1 | convolution fusion | flops 205062144 | bytes 4993029 | tf_op jit(solution)/shard_map/while/body/eval_jaxpr/grtp,pgd->tgrd/dot_general | solution.py:59
  170.5 1.7 fusion.50
  172.2 3.0 %fusion.53 = f32[256,1,6,128]{0,3,2,1:T(8,128)} fusion(f32[512,256,6]{1,0,2:T(8,128)S(1)} %get-tuple-element.407, f32[6,256]{1,0:T(8,128)S(1)} %bitcast.111, pred[256,512]{0,1:T(8,128)(4,1)S(1)} %broadcast_compare_fusion.3, f32[256,1,6,128]{0,3,2,1:T(8,128)} %get-tuple-element.425, f32[256,6]{0,1:T(8,128)S(1)} %get-tuple-element.408, ...), kind=kOutput, calls=%fused_computation.14.clone.1 | convolution fusion | flops 205062144 | bytes 4993029 | tf_op jit(solution)/shard_map/while/body/eval_jaxpr/grtp,pgd->tgrd/dot_general | solution.py:59
  178.0 3.0 %fusion.53 = f32[256,1,6,128]{0,3,2,1:T(8,128)} fusion(f32[512,256,6]{1,0,2:T(8,128)S(1)} %get-tuple-element.407, f32[6,256]{1,0:T(8,128)S(1)} %bitcast.111, pred[256,512]{0,1:T(8,128)(4,1)S(1)} %broadcast_compare_fusion.3, f32[256,1,6,128]{0,3,2,1:T(8,128)} %get-tuple-element.425, f32[256,6]{0,1:T(8,128)S(1)} %get-tuple-element.408, ...), kind=kOutput, calls=%fused_computation.14.clone.1 | convolution fusion | flops 205062144 | bytes 4993029 | tf_op jit(solution)/shard_map/while/body/eval_jaxpr/grtp,pgd->tgrd/dot_general | solution.py:59
  182.1 1.7 fusion.50
  183.8 3.0 %fusion.53 = f32[256,1,6,128]{0,3,2,1:T(8,128)} fusion(f32[512,256,6]{1,0,2:T(8,128)S(1)} %get-tuple-element.407, f32[6,256]{1,0:T(8,128)S(1)} %bitcast.111, pred[256,512]{0,1:T(8,128)(4,1)S(1)} %broadcast_compare_fusion.3, f32[256,1,6,128]{0,3,2,1:T(8,128)} %get-tuple-element.425, f32[256,6]{0,1:T(8,128)S(1)} %get-tuple-element.408, ...), kind=kOutput, calls=%fused_computation.14.clone.1 | convolution fusion | flops 205062144 | bytes 4993029 | tf_op jit(solution)/shard_map/while/body/eval_jaxpr/grtp,pgd->tgrd/dot_general | solution.py:59
  187.8 1.7 fusion.50
  189.5 3.0 %fusion.53 = f32[256,1,6,128]{0,3,2,1:T(8,128)} fusion(f32[512,256,6]{1,0,2:T(8,128)S(1)} %get-tuple-element.407, f32[6,256]{1,0:T(8,128)S(1)} %bitcast.111, pred[256,512]{0,1:T(8,128)(4,1)S(1)} %broadcast_compare_fusion.3, f32[256,1,6,128]{0,3,2,1:T(8,128)} %get-tuple-element.425, f32[256,6]{0,1:T(8,128)S(1)} %get-tuple-element.408, ...), kind=kOutput, calls=%fused_computation.14.clone.1 | convolution fusion | flops 205062144 | bytes 4993029 | tf_op jit(solution)/shard_map/while/body/eval_jaxpr/grtp,pgd->tgrd/dot_general | solution.py:59
  195.3 3.0 %fusion.53 = f32[256,1,6,128]{0,3,2,1:T(8,128)} fusion(f32[512,256,6]{1,0,2:T(8,128)S(1)} %get-tuple-element.407, f32[6,256]{1,0:T(8,128)S(1)} %bitcast.111, pred[256,512]{0,1:T(8,128)(4,1)S(1)} %broadcast_compare_fusion.3, f32[256,1,6,128]{0,3,2,1:T(8,128)} %get-tuple-element.425, f32[256,6]{0,1:T(8,128)S(1)} %get-tuple-element.408, ...), kind=kOutput, calls=%fused_computation.14.clone.1 | convolution fusion | flops 205062144 | bytes 4993029 | tf_op jit(solution)/shard_map/while/body/eval_jaxpr/grtp,pgd->tgrd/dot_general | solution.py:59
  199.4 1.7 fusion.50
  201.1 3.0 %fusion.53 = f32[256,1,6,128]{0,3,2,1:T(8,128)} fusion(f32[512,256,6]{1,0,2:T(8,128)S(1)} %get-tuple-element.407, f32[6,256]{1,0:T(8,128)S(1)} %bitcast.111, pred[256,512]{0,1:T(8,128)(4,1)S(1)} %broadcast_compare_fusion.3, f32[256,1,6,128]{0,3,2,1:T(8,128)} %get-tuple-element.425, f32[256,6]{0,1:T(8,128)S(1)} %get-tuple-element.408, ...), kind=kOutput, calls=%fused_computation.14.clone.1 | convolution fusion | flops 205062144 | bytes 4993029 | tf_op jit(solution)/shard_map/while/body/eval_jaxpr/grtp,pgd->tgrd/dot_general | solution.py:59
  205.2 1.7 fusion.50
  206.9 3.0 %fusion.53 = f32[256,1,6,128]{0,3,2,1:T(8,128)} fusion(f32[512,256,6]{1,0,2:T(8,128)S(1)} %get-tuple-element.407, f32[6,256]{1,0:T(8,128)S(1)} %bitcast.111, pred[256,512]{0,1:T(8,128)(4,1)S(1)} %broadcast_compare_fusion.3, f32[256,1,6,128]{0,3,2,1:T(8,128)} %get-tuple-element.425, f32[256,6]{0,1:T(8,128)S(1)} %get-tuple-element.408, ...), kind=kOutput, calls=%fused_computation.14.clone.1 | convolution fusion | flops 205062144 | bytes 4993029 | tf_op jit(solution)/shard_map/while/body/eval_jaxpr/grtp,pgd->tgrd/dot_general | solution.py:59
  212.7 3.0 %fusion.53 = f32[256,1,6,128]{0,3,2,1:T(8,128)} fusion(f32[512,256,6]{1,0,2:T(8,128)S(1)} %get-tuple-element.407, f32[6,256]{1,0:T(8,128)S(1)} %bitcast.111, pred[256,512]{0,1:T(8,128)(4,1)S(1)} %broadcast_compare_fusion.3, f32[256,1,6,128]{0,3,2,1:T(8,128)} %get-tuple-element.425, f32[256,6]{0,1:T(8,128)S(1)} %get-tuple-element.408, ...), kind=kOutput, calls=%fused_computation.14.clone.1 | convolution fusion | flops 205062144 | bytes 4993029 | tf_op jit(solution)/shard_map/while/body/eval_jaxpr/grtp,pgd->tgrd/dot_general | solution.py:59
  218.4 3.0 %fusion.53 = f32[256,1,6,128]{0,3,2,1:T(8,128)} fusion(f32[512,256,6]{1,0,2:T(8,128)S(1)} %get-tuple-element.407, f32[6,256]{1,0:T(8,128)S(1)} %bitcast.111, pred[256,512]{0,1:T(8,128)(4,1)S(1)} %broadcast_compare_fusion.3, f32[256,1,6,128]{0,3,2,1:T(8,128)} %get-tuple-element.425, f32[256,6]{0,1:T(8,128)S(1)} %get-tuple-element.408, ...), kind=kOutput, calls=%fused_computation.14.clone.1 | convolution fusion | flops 205062144 | bytes 4993029 | tf_op jit(solution)/shard_map/while/body/eval_jaxpr/grtp,pgd->tgrd/dot_general | solution.py:59
  224.2 3.0 %fusion.53 = f32[256,1,6,128]{0,3,2,1:T(8,128)} fusion(f32[512,256,6]{1,0,2:T(8,128)S(1)} %get-tuple-element.407, f32[6,256]{1,0:T(8,128)S(1)} %bitcast.111, pred[256,512]{0,1:T(8,128)(4,1)S(1)} %broadcast_compare_fusion.3, f32[256,1,6,128]{0,3,2,1:T(8,128)} %get-tuple-element.425, f32[256,6]{0,1:T(8,128)S(1)} %get-tuple-element.408, ...), kind=kOutput, calls=%fused_computation.14.clone.1 | convolution fusion | flops 205062144 | bytes 4993029 | tf_op jit(solution)/shard_map/while/body/eval_jaxpr/grtp,pgd->tgrd/dot_general | solution.py:59
  230.0 3.0 %fusion.53 = f32[256,1,6,128]{0,3,2,1:T(8,128)} fusion(f32[512,256,6]{1,0,2:T(8,128)S(1)} %get-tuple-element.407, f32[6,256]{1,0:T(8,128)S(1)} %bitcast.111, pred[256,512]{0,1:T(8,128)(4,1)S(1)} %broadcast_compare_fusion.3, f32[256,1,6,128]{0,3,2,1:T(8,128)} %get-tuple-element.425, f32[256,6]{0,1:T(8,128)S(1)} %get-tuple-element.408, ...), kind=kOutput, calls=%fused_computation.14.clone.1 | convolution fusion | flops 205062144 | bytes 4993029 | tf_op jit(solution)/shard_map/while/body/eval_jaxpr/grtp,pgd->tgrd/dot_general | solution.py:59
  235.8 3.0 %fusion.53 = f32[256,1,6,128]{0,3,2,1:T(8,128)} fusion(f32[512,256,6]{1,0,2:T(8,128)S(1)} %get-tuple-element.407, f32[6,256]{1,0:T(8,128)S(1)} %bitcast.111, pred[256,512]{0,1:T(8,128)(4,1)S(1)} %broadcast_compare_fusion.3, f32[256,1,6,128]{0,3,2,1:T(8,128)} %get-tuple-element.425, f32[256,6]{0,1:T(8,128)S(1)} %get-tuple-element.408, ...), kind=kOutput, calls=%fused_computation.14.clone.1 | convolution fusion | flops 205062144 | bytes 4993029 | tf_op jit(solution)/shard_map/while/body/eval_jaxpr/grtp,pgd->tgrd/dot_general | solution.py:59
  241.6 3.0 %fusion.53 = f32[256,1,6,128]{0,3,2,1:T(8,128)} fusion(f32[512,256,6]{1,0,2:T(8,128)S(1)} %get-tuple-element.407, f32[6,256]{1,0:T(8,128)S(1)} %bitcast.111, pred[256,512]{0,1:T(8,128)(4,1)S(1)} %broadcast_compare_fusion.3, f32[256,1,6,128]{0,3,2,1:T(8,128)} %get-tuple-element.425, f32[256,6]{0,1:T(8,128)S(1)} %get-tuple-element.408, ...), kind=kOutput, calls=%fused_computation.14.clone.1 | convolution fusion | flops 205062144 | bytes 4993029 | tf_op jit(solution)/shard_map/while/body/eval_jaxpr/grtp,pgd->tgrd/dot_general | solution.py:59
  247.3 15.3 %all_to_all.72 = bf16[8,32,768]{2,1,0:T(8,128)(2,1)S(1)} all-to-all(bf16[8,32,768]{2,1,0:T(8,128)(2,1)S(1)} %select_convert_fusion), channel_id=1, replica_groups=mesh['ctx'=32,'head'=8] {'head'}, dimensions={0} | all-to-all | bytes 786432 | tf_op jit(solution)/shard_map/all_to_all | solution.py:98
  (166 shorter events, 39.1 us)
Async XLA Ops:
  6.5 32.6 %copy-start = (f32[64,768]{1,0:T(8,128)S(1)}, f32[64,768]{1,0:T(8,128)}, u32[]{:S(2)}) copy-start(f32[64,768]{1,0:T(8,128)} %param.15) | copy-start | bytes 589828
  6.5 146.6 %copy-start.1 = (s32[64]{0:T(128)S(1)}, s32[64]{0:T(128)}, u32[]{:S(2)}) copy-start(s32[64]{0:T(128)} %param.12) | copy-start | bytes 772
  6.5 80.3 %all-gather.3.cloned.1.call-start = ((), (), s32[]{:S(2)}) async-start(), calls=%async_computation.4 | async-start | bytes 2162688 | tf_op jit(solution)/shard_map/all_gather | solution.py:71
  21.5 131.6 %all-gather.5.cloned.1.call-start = ((), (), s32[]{:S(2)}) async-start(), calls=%async_computation.5 | async-start | bytes 2162688 | tf_op jit(solution)/shard_map/all_gather | solution.py:72
  34.0 12.0 %all-to-all-start.1 = ((bf16[32,8,768]{2,0,1:T(8,128)(2,1)}), bf16[32,8,768]{2,0,1:T(8,128)(2,1)S(1)}, u32[]{:S(2)}, u32[]{:S(2)}) async-start(bf16[32,8,768]{2,0,1:T(8,128)(2,1)} %bitcast.86), calls=%async_computation.1 | async-start | bytes 786432 | tf_op jit(solution)/shard_map/all_to_all | solution.py:22
Sparse Core Ops, SparseCore 0:
  21.7 65.1 all-gather.2
  88.7 64.3 all-gather.4
where the time goes:
time: 271 us; the launch traced here: 270 us
  waiting for transfers between devices  112 us (41%)
  matrix products  75.1 us (28%)
  blocking collectives  39.1 us (14%)
  other arithmetic  17.3 us (6%)
  between operations  13.5 us (5%)
  local copies, waits for them, and re-layouts  8.2 us (3%)
  starting transfers between devices  3.5 us (1%)
    all_gather x1, waiting for transfers between devices, local(): value_piece = lax.all_gather(values_here, 'ctx', axis=0, tiled=True)  66.3 us
    dot_general x16, matrix products, attend(): jnp.einsum('grtp,pgd->tgrd', probs.astype(jnp.bfloat16), value_block.resh...  48 us
    all_gather x1, waiting for transfers between devices, local(): key_piece = lax.all_gather(keys_here, 'ctx', axis=0, tiled=True)  39.6 us
    dot_general x16, matrix products, attend(): jnp.einsum('tgrd,pgd->grtp', grouped, key_block.reshape(width, groups, HD...  26.8 us
    all_to_all x1, blocking collectives, local(): lax.all_to_all(result, 'head', split_axis=0, concat_axis=1, tiled=True)  15.3 us
    all_to_all x1, blocking collectives, local(): lax.all_to_all(keys, 'head', split_axis=1, concat_axis=0, tiled=True)  14.1 us
    reduce_sum x16, other arithmetic, attend(): totals = totals * factor + jnp.sum(probs, axis=-1)  10.7 us
    all_to_all x1, blocking collectives, local(): lax.all_to_all(values, 'head', split_axis=1, concat_axis=0, tiled=True)  9.76 us
  transfers between devices with their start and end apart: 3, of which 3 were waited for; matrix products, arithmetic and copies ran while one was open for 2% of the time, Pallas kernels for 0%

commit v1 on v0

v1 whole, which is shorter than its diff:
```python
import functools
import math

import jax
import jax.numpy as jnp
from jax import lax
from jax.experimental import pallas as pl
from jax.experimental.pallas import tpu as pltpu
from jax.sharding import PartitionSpec as P

HEADS = 48
KVH = 8
HD = 128
SPAN = 128
NZ = 8
NH = 8
RATIO = HEADS // KVH
ROWS = 32
BLOCK = NH * ROWS
GROUP = 4 * BLOCK
FEAT = RATIO * HD
TILE = 256
TILES = 2 * SPAN * RATIO // TILE
VROWS = HD + 16
NEG = -1e30
MESH = pl.DeviceIdType.MESH
K, V = 0, 1


def kernel(
    q_ref, k_ref, v_ref, fold, noisy, noise_step, gate_ref, out_ref,
    q_in, k_buf, v_in, vt_buf, qt, m_s, acc, gate_v, ost,
    a2a_send, a2a_recv, loc_sem, kv_send, kv_recv, out_send, out_recv,
):
    me = lax.axis_index("ctx")
    h = lax.axis_index("head")
    z = lax.div(me, 4)
    x = lax.rem(lax.div(me, 2), 2)
    c = lax.rem(me, 2)
    xh = lax.div(h, 4)
    y = lax.rem(h, 4)

    def ctx_of(dz, x_, c_):
        return lax.rem(z + (dz + NZ), NZ) * 4 + x_ * 2 + c_

    zp, zm = ctx_of(1, x, c), ctx_of(-1, x, c)
    xb, sib = ctx_of(0, 1 - x, c), ctx_of(0, x, 1 - c)
    peers = [lax.rem(h + r, NH) for r in range(1, NH)]

    own_k = pltpu.make_async_copy(
        k_ref.at[:, pl.ds(pl.multiple_of(h * HD, HD), HD)],
        k_buf.at[me, pl.ds(pl.multiple_of(h * ROWS, ROWS), ROWS), :], loc_sem.at[0])
    own_v = pltpu.make_async_copy(
        v_ref.at[:, pl.ds(pl.multiple_of(h * HD, HD), HD)],
        v_in.at[pl.ds(pl.multiple_of(h * ROWS, ROWS), ROWS), :], loc_sem.at[1])
    own_q = pltpu.make_async_copy(
        q_ref.at[:, pl.ds(pl.multiple_of(h * FEAT, FEAT), FEAT)], q_in.at[h], loc_sem.at[2])
    gates = pltpu.make_async_copy(gate_ref, gate_v, loc_sem.at[3])
    own_k.start()
    own_v.start()
    own_q.start()
    gates.start()

    barrier = pltpu.get_barrier_semaphore()
    for peer in peers:
        pl.semaphore_signal(barrier, inc=1, device_id=(me, peer), device_id_type=MESH)
    for other in (zp, zm, xb, sib):
        pl.semaphore_signal(barrier, inc=1, device_id=(other, h), device_id_type=MESH)
    vt_buf[:, HD:, :] = jnp.ones((NZ * 4, VROWS - HD, BLOCK), jnp.bfloat16)
    m_s[...] = jnp.full_like(m_s, NEG)
    acc[...] = jnp.zeros_like(acc)
    pl.semaphore_wait(barrier, NH - 1 + 4)

    def k_copy(i, peer, source):
        return pltpu.make_async_remote_copy(
            k_ref.at[:, pl.ds(pl.multiple_of(peer * HD, HD), HD)],
            k_buf.at[me, pl.ds(pl.multiple_of(source * ROWS, ROWS), ROWS), :],
            a2a_send.at[0, i], a2a_recv.at[0, source], device_id=(me, peer), device_id_type=MESH)

    def v_copy(i, peer, source):
        return pltpu.make_async_remote_copy(
            v_ref.at[:, pl.ds(pl.multiple_of(peer * HD, HD), HD)],
            v_in.at[pl.ds(pl.multiple_of(source * ROWS, ROWS), ROWS), :],
            a2a_send.at[1, i], a2a_recv.at[1, source], device_id=(me, peer), device_id_type=MESH)

    def q_copy(i, peer, source):
        return pltpu.make_async_remote_copy(
            q_ref.at[:, pl.ds(pl.multiple_of(peer * FEAT, FEAT), FEAT)], q_in.at[source],
            a2a_send.at[2, i], a2a_recv.at[2, source], device_id=(me, peer), device_id_type=MESH)

    for i, peer in enumerate(peers):
        k_copy(i, peer, h).start()
    for i, peer in enumerate(peers):
        v_copy(i, peer, h).start()
    for i, peer in enumerate(peers):
        q_copy(i, peer, h).start()

    sent = []

    def block_copy(half, block, target, send):
        ref = k_buf.at[block] if half == K else vt_buf.at[block, pl.ds(0, HD), :]
        return pltpu.make_async_remote_copy(
            ref, ref, kv_send.at[send], kv_recv.at[half, block],
            device_id=(target, h), device_id_type=MESH)

    def send(half, block, *targets):
        for target in targets:
            block_copy(half, block, target, len(sent)).start()
            sent.append((half, block, target))

    def arrived(half, block):
        block_copy(half, block, sib, 0).wait_recv()

    own = lambda d: ctx_of(d, x, c)
    oth = lambda d: ctx_of(d, 1 - x, c)

    own_k.wait()
    for i, peer in enumerate(peers):
        k_copy(i, peer, peer).wait_recv()
    send(K, me, xb, zp, zm, sib)
    own_v.wait()
    for i, peer in enumerate(peers):
        v_copy(i, peer, peer).wait_recv()
    vt_buf[me, :HD, :] = v_in[...].astype(jnp.float32).T.astype(jnp.bfloat16)
    send(V, me, xb, zp, zm, sib)

    arrived(K, oth(0))
    send(K, oth(0), zp, zm, sib)
    arrived(V, oth(0))
    send(V, oth(0), sib)

    def own_came(d):
        for sign, onward in ((-1, zp), (1, zm)):
            block = own(sign * d)
            arrived(K, block)
            send(K, block, *((onward,) if d < 3 or sign < 0 else ()), sib)
        for sign, onward in ((-1, zp), (1, zm)):
            block = own(sign * d)
            arrived(V, block)
            send(V, block, *((onward,) if d < 3 or sign > 0 else ()), xb, sib)

    def oth_came(d):
        for sign, onward in ((-1, zp), (1, zm)):
            block = oth(sign * d)
            arrived(K, block)
            send(K, block, *((onward,) if d < 3 else ()), sib)
        for sign in (-1, 1):
            block = oth(sign * d)
            arrived(V, block)
            send(V, block, sib)

    def own_last():
        arrived(K, own(4))
        send(K, own(4), xb, sib)
        arrived(V, own(4))
        send(V, own(4), xb, sib)

    def oth_last():
        arrived(K, oth(4))
        send(K, oth(4), sib)
        arrived(V, oth(4))
        send(V, oth(4), sib)

    def sibling(d):
        for x_ in (0, 1):
            for half in (K, V):
                arrived(half, ctx_of(d, x_, 1 - c))

    own_came(1)

    own_q.wait()
    for i, peer in enumerate(peers):
        q_copy(i, peer, peer).wait_recv()
    factor = math.log2(math.e) / math.sqrt(HD)
    spans = [1 - xh, xh]
    for slot in range(2):
        for j in range(RATIO):
            part = q_in[pl.ds(spans[slot] * 4, 4), :, j * HD:(j + 1) * HD].reshape(SPAN, HD)
            scaled = (part.astype(jnp.float32) * factor).T
            high = scaled.astype(jnp.bfloat16)
            low = (scaled - high.astype(jnp.float32)).astype(jnp.bfloat16)
            at = (slot * RATIO + j) * HD
            qt[0:HD, at:at + HD] = high
            qt[HD:2 * HD, at:at + HD] = low

    my_order = [fold[2 * me + s] for s in spans]
    gate_rows = [gate_v.at[pl.ds(noise_step[o], 1), :] for o in my_order]
    live = [noisy[o] == 1 for o in my_order]

    def work(zq, done=None):
        keys = k_buf[pl.ds(zq * 4, 4)].reshape(GROUP, HD)
        keys = jnp.concatenate([keys, keys], axis=1)
        values = jnp.concatenate([vt_buf[zq * 4 + i] for i in range(4)], axis=1)
        count = GROUP // SPAN
        orders = [fold[zq * count + i] for i in range(count)]
        hide = [
            [jnp.where(o <= mine, jnp.float32(0), jnp.float32(NEG)) for o in orders]
            for mine in my_order
        ]

        def score(t):
            return jnp.dot(keys, qt[:, t * TILE:(t + 1) * TILE], preferred_element_type=jnp.float32)

        def soften(t, s):
            cols = slice(t * TILE, (t + 1) * TILE)
            bias = hide[t // (TILES // 2)]
            before = m_s[0:1, cols]
            top = before
            for i in range(count):
                top = jnp.maximum(top, jnp.max(s[i * SPAN:(i + 1) * SPAN], axis=0, keepdims=True) + bias[i])
            probs = [
                jnp.exp2(s[i * SPAN:(i + 1) * SPAN] - (top - 2 * bias[i])).astype(jnp.bfloat16)
                for i in range(count)
            ]
            m_s[0:1, cols] = top
            return jnp.concatenate(probs, axis=0), jnp.exp2(before - top)

        def add(t, probs, alpha):
            cols = slice(t * TILE, (t + 1) * TILE)
            total = acc[:, cols] * alpha + jnp.dot(values, probs, preferred_element_type=jnp.float32)
            if done is None:
                acc[:, cols] = total
            else:
                done(t, total)

        s = score(0)
        held = None
        for t in range(TILES):
            following = score(t + 1) if t + 1 < TILES else None
            if held is not None:
                add(t - 1, *held)
            held = soften(t, s)
            s = following
        add(TILES - 1, *held)

    events = {
        0: [lambda: oth_came(1)],
        1: [lambda: own_came(2)],
        2: [lambda: oth_came(2)],
        3: [lambda: own_came(3)],
        4: [lambda: oth_came(3), own_last],
        6: [oth_last],
    }

    sibling(0)

    def step(i, carry):
        for at, todo in events.items():
            if at < NZ - 1:
                @pl.when(i == at)
                def _():
                    for f in todo:
                        f()
        for d in (1, 2, 3):
            @pl.when(i == 2 * d - 1)
            def _():
                sibling(d)
                sibling(-d)
        near = lax.div(i + 1, 2)
        d = jnp.where(lax.rem(i, 2) == 1, near, NZ - near)
        work(lax.rem(z + d, NZ))
        return carry

    lax.fori_loop(0, NZ - 1, step, 0)
    sibling(4)

    results = []

    def result_copy(t, target, part, i):
        jp = t % 3
        src = ost.at[t, pl.ds(pl.multiple_of(part * ROWS, ROWS), ROWS), :]
        dst = out_ref.at[:, pl.ds(pl.multiple_of(h * FEAT + jp * TILE, TILE), TILE)]
        return pltpu.make_async_remote_copy(
            src, dst, out_send.at[i], out_recv.at[h, jp],
            device_id=(me, target), device_id_type=MESH)

    def own_result(t):
        jp = t % 3
        return pltpu.make_async_copy(
            ost.at[t, pl.ds(pl.multiple_of(y * ROWS, ROWS), ROWS), :],
            out_ref.at[:, pl.ds(pl.multiple_of(h * FEAT + jp * TILE, TILE), TILE)],
            loc_sem.at[4 + jp])

    gates.wait()

    def done(t, total):
        slot = t // 3
        jp = t % 3
        scaled = total[:HD] * (1.0 / total[HD:HD + 1])
        for jj in range(2):
            j = 2 * jp + jj
            rows = scaled[:, jj * HD:(jj + 1) * HD].T
            rows = rows * gate_rows[slot][:, j * HD:(j + 1) * HD]
            rows = jnp.where(live[slot], rows, jnp.float32(0))
            ost[t, :, jj * HD:(jj + 1) * HD] = rows.astype(jnp.bfloat16)
        for r in range(4):
            part = lax.rem(y + r, 4)
            if slot == 1 and r == 0:
                own_result(t).start()
                continue
            i = len(results)
            target = spans[slot] * 4 + part
            result_copy(t, target, part, i).start()
            results.append((t, target, part))

    work(lax.rem(z + 4, NZ), done)

    for jp in range(3):
        own_result(3 + jp).wait()
    for i, (t, target, part) in enumerate(results):
        result_copy(t, target, part, i).wait_send()
    for i, peer in enumerate(peers):
        k_copy(i, peer, h).wait_send()
        v_copy(i, peer, h).wait_send()
        q_copy(i, peer, h).wait_send()
    for i, (half, block, target) in enumerate(sent):
        block_copy(half, me, sib, i).wait_send()
    for peer in peers:
        for jp in range(3):
            pltpu.make_async_remote_copy(
                ost.at[0, pl.ds(0, ROWS), :],
                out_ref.at[:, pl.ds(pl.multiple_of(peer * FEAT + jp * TILE, TILE), TILE)],
                out_send.at[0], out_recv.at[peer, jp],
                device_id=(me, peer), device_id_type=MESH).wait_recv()


def local(queries, keys, values, fold_map, noisy, noise_step, gate_table):
    hbm = pl.BlockSpec(memory_space=pl.ANY)
    smem = pl.BlockSpec(memory_space=pltpu.SMEM)
    width = 2 * SPAN * RATIO
    blocks = NZ * 4
    return pl.pallas_call(
        kernel,
        out_shape=jax.ShapeDtypeStruct(queries.shape, queries.dtype),
        in_specs=[hbm, hbm, hbm, smem, smem, smem, hbm],
        out_specs=hbm,
        scratch_shapes=[
            pltpu.VMEM((NH, ROWS, FEAT), jnp.bfloat16),
            pltpu.VMEM((blocks, BLOCK, HD), jnp.bfloat16),
            pltpu.VMEM((BLOCK, HD), jnp.bfloat16),
            pltpu.VMEM((blocks, VROWS, BLOCK), jnp.bfloat16),
            pltpu.VMEM((2 * HD, width), jnp.bfloat16),
            pltpu.VMEM((8, width), jnp.float32),
            pltpu.VMEM((VROWS, width), jnp.float32),
            pltpu.VMEM(gate_table.shape, jnp.float32),
            pltpu.VMEM((TILES, SPAN, TILE), jnp.bfloat16),
            pltpu.SemaphoreType.DMA((3, NH)),
            pltpu.SemaphoreType.DMA((3, NH)),
            pltpu.SemaphoreType.DMA((8,)),
            pltpu.SemaphoreType.DMA((64,)),
            pltpu.SemaphoreType.DMA((2, blocks)),
            pltpu.SemaphoreType.DMA((24,)),
            pltpu.SemaphoreType.DMA((NH, 3)),
        ],
        compiler_params=pltpu.CompilerParams(
            collective_id=0, has_side_effects=True, vmem_limit_bytes=48 * 2**20
        ),
        cost_estimate=pl.CostEstimate(
            flops=2 * 2 * width * 8192 * HD, bytes_accessed=2**20, transcendentals=width * 8192
        ),
    )(queries, keys, values, fold_map, noisy, noise_step, gate_table)


def solution(mesh):
    placed = (
        P(("ctx", "head"), None),
        P(("ctx", "head"), None),
        P(("ctx", "head"), None),
        P(),
        P(),
        P(),
        P(None, "head"),
    )
    return jax.shard_map(
        local, mesh=mesh, in_specs=placed, out_specs=P(("ctx", "head"), None), check_vma=False
    )
```

time: 271 us -> 61.2 us (0.23)
  waiting for transfers between devices: 112 us -> 0 us
  matrix products: 75.1 us -> 0 us
  Pallas kernels: 0 us -> 54.5 us
  blocking collectives: 39.1 us -> 0 us
  other arithmetic: 17.3 us -> 0 us
  between operations: 13.5 us -> 0.02 us
  starting transfers between devices: 3.5 us -> 0 us
    all_gather x2 -> x0, waiting for transfers between devices: 106 us -> none  [the longest x1 66.3 us: local(): value_piece = lax.all_gather(values_here, 'ctx', axis=0, tiled=True)]
    dot_general x33 -> x0, matrix products: 75.1 us -> none  [the longest x16 48 us: attend(): jnp.einsum('grtp,pgd->tgrd', probs.astype(jnp.bfloat16), value_block.resh...]
    pallas_call x0 -> x1, Pallas kernels: none -> 54.5 us  [local(): pl.pallas_call(kernel, out_shape=jax.ShapeDtypeStruct(queries.shape, quer...]
    all_to_all x3 -> x0, blocking collectives: 39.1 us -> none  [the longest x1 15.3 us: local(): lax.all_to_all(result, 'head', split_axis=0, concat_axis=1, tiled=True)]
    reduce_sum x33 -> x0, other arithmetic: 13.1 us -> none  [the longest x16 10.7 us: attend(): totals = totals * factor + jnp.sum(probs, axis=-1)]
    all_to_all x1 -> x0, waiting for transfers between devices: 6.43 us -> none  [local(): lax.all_to_all(queries, 'head', split_axis=1, concat_axis=0, tiled=True)]
    unnamed x5 -> x15, local copies, waits for them, and re-layouts: 0.81 us -> 6.31 us
    all_to_all x4 -> x0, local copies, waits for them, and re-layouts: 4.29 us -> none  [the longest x1 1.77 us: local(): lax.all_to_all(queries, 'head', split_axis=1, concat_axis=0, tiled=True)]
  transfers between devices with their start and end apart: 3 -> 0, of which waited for: 3 -> 0; matrix products, arithmetic and copies ran while one was open for 2% -> 0% of each run, Pallas kernels for 0% -> 0%
where the time goes in v1:
time: 61.2 us; the launch traced here: 60.9 us
  Pallas kernels  54.5 us (89%)
  local copies, waits for them, and re-layouts  6.31 us (10%)
    pallas_call x1, Pallas kernels, local(): pl.pallas_call(kernel, out_shape=jax.ShapeDtypeStruct(queries.shape, quer...  54.5 us
    unnamed x15, local copies, waits for them, and re-layouts  6.31 us

profile of v1, /device:TPU:1, one launch (start us, length us, event | category | flops | bytes accessed | tf_op | source)
XLA Modules:
  0.0 60.9 jit_solution(221964869977030834)
XLA Ops:
  0.0 0.0 copy-start
  0.0 1.0 %copy-done = bf16[32,6144]{1,0:T(8,128)(2,1)S(1)} copy-done((bf16[32,6144]{1,0:T(8,128)(2,1)S(1)}, bf16[32,6144]{1,0:T(8,128)(2,1)}, u32[]{:S(2)}) %copy-start) | copy-done | bytes 393240
  1.0 0.0 copy-start.1
  1.0 0.9 %copy-done.1 = f32[64,768]{1,0:T(8,128)S(1)} copy-done((f32[64,768]{1,0:T(8,128)S(1)}, f32[64,768]{1,0:T(8,128)}, u32[]{:S(2)}) %copy-start.1) | copy-done | bytes 196632
  1.9 0.0 copy-start.2
  1.9 0.8 %copy-done.2 = bf16[32,1024]{1,0:T(8,128)(2,1)S(1)} copy-done((bf16[32,1024]{1,0:T(8,128)(2,1)S(1)}, bf16[32,1024]{1,0:T(8,128)(2,1)}, u32[]{:S(2)}) %copy-start.2) | copy-done | bytes 65560
  2.8 0.0 copy-start.3
  2.8 0.8 %copy-done.3 = bf16[32,1024]{1,0:T(8,128)(2,1)S(1)} copy-done((bf16[32,1024]{1,0:T(8,128)(2,1)S(1)}, bf16[32,1024]{1,0:T(8,128)(2,1)}, u32[]{:S(2)}) %copy-start.3) | copy-done | bytes 65560
  3.6 0.0 copy-start.4
  3.6 0.7 %copy-done.4 = s32[64]{0:T(128)S(1)} copy-done((s32[64]{0:T(128)S(1)}, s32[64]{0:T(128)}, u32[]{:S(2)}) %copy-start.4) | copy-done | bytes 280
  4.3 0.0 copy-start.5
  4.3 0.7 %copy-done.5 = s32[64]{0:T(128)S(1)} copy-done((s32[64]{0:T(128)S(1)}, s32[64]{0:T(128)}, u32[]{:S(2)}) %copy-start.5) | copy-done | bytes 280
  4.9 0.0 copy-start.6
  4.9 0.7 %copy-done.6 = s32[64]{0:T(128)S(1)} copy-done((s32[64]{0:T(128)S(1)}, s32[64]{0:T(128)}, u32[]{:S(2)}) %copy-start.6) | copy-done | bytes 280
  5.6 54.5 %shard_map.73 = bf16[32,6144]{1,0:T(8,128)(2,1)S(1)} custom-call(bf16[32,6144]{1,0:T(8,128)(2,1)S(1)} %copy-done, bf16[32,1024]{1,0:T(8,128)(2,1)S(1)} %copy-done.2, bf16[32,1024]{1,0:T(8,128)(2,1)S(1)} %copy-done.3, s32[64]{0:T(128)S(1)} %copy-done.4, s32[64]{0:T(128)S(1)} %copy-done.5, s32[64]{0:T(128)S(1)} %copy-done.6, f32[64,768]{1,0:T(8,128)S(1)} %copy-done.1), custom_call_target="tpu_custom_call" | custom-call | flops 6442450944 | bytes 1048576 | tf_op jit(solution)/shard_map/pallas_call | solution.py:332
  60.1 0.7 %copy.9 = bf16[32,6144]{1,0:T(8,128)(2,1)} copy(bf16[32,6144]{1,0:T(8,128)(2,1)S(1)} %shard_map.73) | data formatting | bytes 786432
Async XLA Ops:
  0.0 1.0 %copy-start = (bf16[32,6144]{1,0:T(8,128)(2,1)S(1)}, bf16[32,6144]{1,0:T(8,128)(2,1)}, u32[]{:S(2)}) copy-start(bf16[32,6144]{1,0:T(8,128)(2,1)} %q_ref.1) | copy-start | bytes 1179652
  1.0 0.9 %copy-start.1 = (f32[64,768]{1,0:T(8,128)S(1)}, f32[64,768]{1,0:T(8,128)}, u32[]{:S(2)}) copy-start(f32[64,768]{1,0:T(8,128)} %gate_ref.1) | copy-start | bytes 589828
  1.9 0.8 %copy-start.2 = (bf16[32,1024]{1,0:T(8,128)(2,1)S(1)}, bf16[32,1024]{1,0:T(8,128)(2,1)}, u32[]{:S(2)}) copy-start(bf16[32,1024]{1,0:T(8,128)(2,1)} %k_ref.1) | copy-start | bytes 196612
  2.8 0.8 %copy-start.3 = (bf16[32,1024]{1,0:T(8,128)(2,1)S(1)}, bf16[32,1024]{1,0:T(8,128)(2,1)}, u32[]{:S(2)}) copy-start(bf16[32,1024]{1,0:T(8,128)(2,1)} %v_ref.1) | copy-start | bytes 196612
  3.6 0.7 %copy-start.4 = (s32[64]{0:T(128)S(1)}, s32[64]{0:T(128)}, u32[]{:S(2)}) copy-start(s32[64]{0:T(128)} %fold.1) | copy-start | bytes 772
  4.3 0.7 %copy-start.5 = (s32[64]{0:T(128)S(1)}, s32[64]{0:T(128)}, u32[]{:S(2)}) copy-start(s32[64]{0:T(128)} %noisy.1) | copy-start | bytes 772
  4.9 0.7 %copy-start.6 = (s32[64]{0:T(128)S(1)}, s32[64]{0:T(128)}, u32[]{:S(2)}) copy-start(s32[64]{0:T(128)} %noise_step.1) | copy-start | bytes 772

commit v2 on v1

v2 whole, which is shorter than its diff:
```python
import functools
import math

import jax
import jax.numpy as jnp
from jax import lax
from jax.experimental import pallas as pl
from jax.experimental.pallas import tpu as pltpu
from jax.sharding import PartitionSpec as P

HEADS = 48
KVH = 8
HD = 128
SPAN = 128
NZ = 8
NH = 8
RATIO = HEADS // KVH
ROWS = 32
BLOCK = NH * ROWS
GROUP = 4 * BLOCK
FEAT = RATIO * HD
TILE = 256
TILES = 2 * SPAN * RATIO // TILE
VROWS = HD + 16
NEG = -1e30
MESH = pl.DeviceIdType.MESH
K, V = 0, 1


def kernel(
    q_ref, k_ref, v_ref, fold, noisy, noise_step, gate_ref, out_ref,
    q_in, k_buf, v_in, vt_buf, qt, m_s, acc, gate_v, ost,
    a2a_send, a2a_recv, loc_sem, kv_send, kv_recv, out_send, out_recv,
):
    me = lax.axis_index("ctx")
    h = lax.axis_index("head")
    z = lax.div(me, 4)
    x = lax.rem(lax.div(me, 2), 2)
    c = lax.rem(me, 2)
    xh = lax.div(h, 4)
    y = lax.rem(h, 4)

    def ctx_of(dz, x_, c_):
        return lax.rem(z + (dz + NZ), NZ) * 4 + x_ * 2 + c_

    zp, zm = ctx_of(1, x, c), ctx_of(-1, x, c)
    xb, sib = ctx_of(0, 1 - x, c), ctx_of(0, x, 1 - c)
    peers = [(me, xh * 4 + lax.rem(y + r, 4), 4 + lax.rem(y + r, 4), 4 + y) for r in range(1, 4)]
    peers += [(xb, (1 - xh) * 4 + lax.rem(y + r, 4), lax.rem(y + r, 4), y) for r in range(4)]
    mine = 4 + y

    own_k = pltpu.make_async_copy(
        k_ref.at[:, pl.ds(pl.multiple_of(h * HD, HD), HD)],
        k_buf.at[me, pl.ds(pl.multiple_of(mine * ROWS, ROWS), ROWS), :], loc_sem.at[0])
    own_v = pltpu.make_async_copy(
        v_ref.at[:, pl.ds(pl.multiple_of(h * HD, HD), HD)],
        v_in.at[pl.ds(pl.multiple_of(mine * ROWS, ROWS), ROWS), :], loc_sem.at[1])
    own_q = pltpu.make_async_copy(
        q_ref.at[:, pl.ds(pl.multiple_of(h * FEAT, FEAT), FEAT)], q_in.at[mine], loc_sem.at[2])
    gates = pltpu.make_async_copy(gate_ref, gate_v, loc_sem.at[3])
    own_k.start()
    own_v.start()
    own_q.start()
    gates.start()

    barrier = pltpu.get_barrier_semaphore()
    for ctx, head, _, _ in peers:
        pl.semaphore_signal(barrier, inc=1, device_id=(ctx, head), device_id_type=MESH)
    for other in (zp, zm, xb, sib):
        pl.semaphore_signal(barrier, inc=1, device_id=(other, h), device_id_type=MESH)
    vt_buf[:, HD:, :] = jnp.ones((NZ * 4, VROWS - HD, BLOCK), jnp.bfloat16)
    m_s[...] = jnp.full_like(m_s, NEG)
    acc[...] = jnp.zeros_like(acc)
    pl.semaphore_wait(barrier, NH - 1 + 4)

    def k_copy(i, slot, block):
        ctx, head, _, _ = peers[i]
        return pltpu.make_async_remote_copy(
            k_ref.at[:, pl.ds(pl.multiple_of(head * HD, HD), HD)],
            k_buf.at[block, pl.ds(pl.multiple_of(slot * ROWS, ROWS), ROWS), :],
            a2a_send.at[0, i], a2a_recv.at[0, slot], device_id=(ctx, head), device_id_type=MESH)

    def v_copy(i, slot, block):
        ctx, head, _, _ = peers[i]
        return pltpu.make_async_remote_copy(
            v_ref.at[:, pl.ds(pl.multiple_of(head * HD, HD), HD)],
            v_in.at[pl.ds(pl.multiple_of(slot * ROWS, ROWS), ROWS), :],
            a2a_send.at[1, i], a2a_recv.at[1, slot], device_id=(ctx, head), device_id_type=MESH)

    def q_copy(i, slot, block):
        ctx, head, _, _ = peers[i]
        return pltpu.make_async_remote_copy(
            q_ref.at[:, pl.ds(pl.multiple_of(head * FEAT, FEAT), FEAT)], q_in.at[slot],
            a2a_send.at[2, i], a2a_recv.at[2, slot], device_id=(ctx, head), device_id_type=MESH)

    for copy in (k_copy, v_copy, q_copy):
        for i, peer in enumerate(peers):
            copy(i, peer[3], peer[0]).start()

    sent = []

    def block_copy(half, block, target, send):
        ref = k_buf.at[block] if half == K else vt_buf.at[block, pl.ds(0, HD), :]
        return pltpu.make_async_remote_copy(
            ref, ref, kv_send.at[send], kv_recv.at[half, block],
            device_id=(target, h), device_id_type=MESH)

    def send(half, block, *targets):
        for target in targets:
            block_copy(half, block, target, len(sent)).start()
            sent.append((half, block, target))

    def arrived(half, block):
        block_copy(half, block, sib, 0).wait_recv()

    own = lambda d: ctx_of(d, x, c)
    oth = lambda d: ctx_of(d, 1 - x, c)

    def come(half, block, *targets):
        arrived(half, block)
        send(half, block, *targets, sib)

    own_k.wait()
    for i, peer in enumerate(peers):
        k_copy(i, peer[2], me).wait_recv()
    send(K, me, xb, zp, zm, sib)
    own_v.wait()
    for i, peer in enumerate(peers):
        v_copy(i, peer[2], me).wait_recv()
    vt_buf[me, :HD, :] = v_in[...].astype(jnp.float32).T.astype(jnp.bfloat16)
    send(V, me, xb, zp, zm, sib)

    def own_k_came(d):
        come(K, own(-d), zp, xb)
        come(K, own(d), *((zm,) if d < 3 else ()), xb)

    def own_v_came(d):
        come(V, own(-d), *((zp,) if d < 3 else ()))
        come(V, own(d), zm)

    def oth_v_came(d):
        come(V, oth(-d), *((zp,) if d < 3 else ()))
        come(V, oth(d), *((zm,) if d < 3 else ()))

    def sibling(d):
        for x_ in (0, 1):
            for half in (K, V):
                arrived(half, ctx_of(d, x_, 1 - c))

    come(K, oth(0))
    own_k_came(1)
    come(V, oth(0), zp, zm)
    own_v_came(1)

    own_q.wait()
    for i, peer in enumerate(peers):
        q_copy(i, peer[2], me).wait_recv()
    factor = math.log2(math.e) / math.sqrt(HD)
    for slot in range(2):
        for j in range(RATIO):
            part = q_in[slot * 4:slot * 4 + 4, :, j * HD:(j + 1) * HD].reshape(SPAN, HD)
            scaled = (part.astype(jnp.float32) * factor).T
            high = scaled.astype(jnp.bfloat16)
            low = (scaled - high.astype(jnp.float32)).astype(jnp.bfloat16)
            at = (slot * RATIO + j) * HD
            qt[0:HD, at:at + HD] = high
            qt[HD:2 * HD, at:at + HD] = low

    my_order = [fold[2 * xb + 1 - xh], fold[2 * me + xh]]
    gate_rows = [gate_v.at[pl.ds(noise_step[o], 1), :] for o in my_order]
    live = [noisy[o] == 1 for o in my_order]

    def work(zq, slot, done=None):
        keys = k_buf[pl.ds(zq * 4, 4)].reshape(GROUP, HD)
        keys = jnp.concatenate([keys, keys], axis=1)
        values = jnp.concatenate([vt_buf[zq * 4 + i] for i in range(4)], axis=1)
        count = GROUP // SPAN
        first = 8 * zq
        orders = []
        for i in range(4):
            orders.append(fold[first + 2 * ((i + 2) % 4) + 1 - xh])
            orders.append(fold[first + 2 * i + xh])
        slots = (0, 1) if slot is None else (slot,)
        hide = []
        for a in slots:
            order = my_order[a] if isinstance(a, int) else jnp.where(a == 0, my_order[0], my_order[1])
            hide.append([jnp.where(o <= order, jnp.float32(0), jnp.float32(NEG)) for o in orders])
        tiles = (TILES // 2) * len(slots)

        def cols(t):
            if slot is None:
                return slice(t * TILE, (t + 1) * TILE)
            return pl.ds(pl.multiple_of((slot * (TILES // 2) + t) * TILE, TILE), TILE)

        def score(t):
            return jnp.dot(keys, qt[:, cols(t)], preferred_element_type=jnp.float32)

        def soften(t, s):
            bias = hide[t // (TILES // 2)]
            before = m_s[0:1, cols(t)]
            top = before
            for i in range(count):
                top = jnp.maximum(top, jnp.max(s[i * SPAN:(i + 1) * SPAN], axis=0, keepdims=True) + bias[i])
            probs = [
                jnp.exp2(s[i * SPAN:(i + 1) * SPAN] - (top - 2 * bias[i])).astype(jnp.bfloat16)
                for i in range(count)
            ]
            m_s[0:1, cols(t)] = top
            return jnp.concatenate(probs, axis=0), jnp.exp2(before - top)

        def add(t, probs, alpha):
            total = acc[:, cols(t)] * alpha + jnp.dot(values, probs, preferred_element_type=jnp.float32)
            if done is None:
                acc[:, cols(t)] = total
            else:
                done(t, total)

        s = score(0)
        held = None
        for t in range(tiles):
            following = score(t + 1) if t + 1 < tiles else None
            if held is not None:
                add(t - 1, *held)
            held = soften(t, s)
            s = following
        add(tiles - 1, *held)

    events = {
        0: lambda: sibling(0),
        1: lambda: (own_k_came(2), come(K, oth(1))),
        2: lambda: (oth_v_came(1), come(K, oth(-1)), sibling(1), sibling(-1)),
        3: lambda: (own_v_came(2), come(K, oth(2))),
        4: lambda: (own_k_came(3), come(K, oth(-2))),
        5: lambda: oth_v_came(2),
        6: lambda: (sibling(2), sibling(-2)),
        7: lambda: (own_v_came(3), come(K, oth(3))),
        8: lambda: (come(K, own(4), xb), come(K, oth(-3))),
        9: lambda: oth_v_came(3),
        10: lambda: (come(V, own(4), xb), sibling(3), sibling(-3)),
        12: lambda: come(K, oth(4)),
        13: lambda: come(V, oth(4)),
    }

    def step(u, carry):
        for at, todo in events.items():
            @pl.when(u == at)
            def _():
                todo()
        i = lax.div(u, 2)
        near = lax.div(i + 1, 2)
        d = jnp.where(lax.rem(i, 2) == 1, near, NZ - near)
        work(lax.rem(z + d, NZ), lax.rem(u, 2))
        return carry

    lax.fori_loop(0, 2 * (NZ - 1), step, 0)
    sibling(4)

    results = []

    def result_copy(t, part, i):
        jp = t % 3
        ctx, base = (xb, (1 - xh) * 4) if t < 3 else (me, xh * 4)
        return pltpu.make_async_remote_copy(
            ost.at[t, pl.ds(pl.multiple_of(part * ROWS, ROWS), ROWS), :],
            out_ref.at[:, pl.ds(pl.multiple_of(h * FEAT + jp * TILE, TILE), TILE)],
            out_send.at[i], out_recv.at[h, jp],
            device_id=(ctx, base + part), device_id_type=MESH)

    def own_result(t):
        jp = t % 3
        return pltpu.make_async_copy(
            ost.at[t, pl.ds(pl.multiple_of(y * ROWS, ROWS), ROWS), :],
            out_ref.at[:, pl.ds(pl.multiple_of(h * FEAT + jp * TILE, TILE), TILE)],
            loc_sem.at[4 + jp])

    gates.wait()

    def done(t, total):
        slot = t // 3
        jp = t % 3
        scaled = total[:HD] * (1.0 / total[HD:HD + 1])
        for jj in range(2):
            j = 2 * jp + jj
            rows = scaled[:, jj * HD:(jj + 1) * HD].T
            rows = rows * gate_rows[slot][:, j * HD:(j + 1) * HD]
            rows = jnp.where(live[slot], rows, jnp.float32(0))
            ost[t, :, jj * HD:(jj + 1) * HD] = rows.astype(jnp.bfloat16)
        for r in range(4):
            part = lax.rem(y + r, 4)
            if slot == 1 and r == 0:
                own_result(t).start()
                continue
            result_copy(t, part, len(results)).start()
            results.append((t, part))

    work(lax.rem(z + 4, NZ), None, done)

    for jp in range(3):
        own_result(3 + jp).wait()
    for i, (t, part) in enumerate(results):
        result_copy(t, part, i).wait_send()
    for i, peer in enumerate(peers):
        for copy in (k_copy, v_copy, q_copy):
            copy(i, peer[3], peer[0]).wait_send()
    for i, (half, block, target) in enumerate(sent):
        block_copy(half, me, sib, i).wait_send()
    for ctx, head, _, _ in peers:
        for jp in range(3):
            pltpu.make_async_remote_copy(
                ost.at[0, pl.ds(0, ROWS), :],
                out_ref.at[:, pl.ds(pl.multiple_of(head * FEAT + jp * TILE, TILE), TILE)],
                out_send.at[0], out_recv.at[head, jp],
                device_id=(ctx, head), device_id_type=MESH).wait_recv()


def local(queries, keys, values, fold_map, noisy, noise_step, gate_table):
    hbm = pl.BlockSpec(memory_space=pl.ANY)
    smem = pl.BlockSpec(memory_space=pltpu.SMEM)
    width = 2 * SPAN * RATIO
    blocks = NZ * 4
    return pl.pallas_call(
        kernel,
        out_shape=jax.ShapeDtypeStruct(queries.shape, queries.dtype),
        in_specs=[hbm, hbm, hbm, smem, smem, smem, hbm],
        out_specs=hbm,
        scratch_shapes=[
            pltpu.VMEM((NH, ROWS, FEAT), jnp.bfloat16),
            pltpu.VMEM((blocks, BLOCK, HD), jnp.bfloat16),
            pltpu.VMEM((BLOCK, HD), jnp.bfloat16),
            pltpu.VMEM((blocks, VROWS, BLOCK), jnp.bfloat16),
            pltpu.VMEM((2 * HD, width), jnp.bfloat16),
            pltpu.VMEM((8, width), jnp.float32),
            pltpu.VMEM((VROWS, width), jnp.float32),
            pltpu.VMEM(gate_table.shape, jnp.float32),
            pltpu.VMEM((TILES, SPAN, TILE), jnp.bfloat16),
            pltpu.SemaphoreType.DMA((3, NH)),
            pltpu.SemaphoreType.DMA((3, NH)),
            pltpu.SemaphoreType.DMA((8,)),
            pltpu.SemaphoreType.DMA((64,)),
            pltpu.SemaphoreType.DMA((2, blocks)),
            pltpu.SemaphoreType.DMA((24,)),
            pltpu.SemaphoreType.DMA((NH, 3)),
        ],
        compiler_params=pltpu.CompilerParams(
            collective_id=0, has_side_effects=True, vmem_limit_bytes=60 * 2**20
        ),
        cost_estimate=pl.CostEstimate(
            flops=2 * 2 * width * 8192 * HD, bytes_accessed=2**20, transcendentals=width * 8192
        ),
    )(queries, keys, values, fold_map, noisy, noise_step, gate_table)


def solution(mesh):
    placed = (
        P(("ctx", "head"), None),
        P(("ctx", "head"), None),
        P(("ctx", "head"), None),
        P(),
        P(),
        P(),
        P(None, "head"),
    )
    return jax.shard_map(
        local, mesh=mesh, in_specs=placed, out_specs=P(("ctx", "head"), None), check_vma=False
    )
```

time: 61.2 us -> 57.4 us (0.938)
  local copies, waits for them, and re-layouts: 6.31 us -> 1.77 us
  Pallas kernels: 54.5 us -> 55.5 us
    unnamed x15 -> x1, local copies, waits for them, and re-layouts: 6.31 us -> 1.77 us
    pallas_call x1, Pallas kernels: 54.5 us -> 55.5 us  [local(): pl.pallas_call(kernel, out_shape=jax.ShapeDtypeStruct(queries.shape, quer...]
where the time goes in v2:
time: 57.4 us; the launch traced here: 57.3 us
  Pallas kernels  55.5 us (97%)
  local copies, waits for them, and re-layouts  1.77 us (3%)
    pallas_call x1, Pallas kernels, local(): pl.pallas_call(kernel, out_shape=jax.ShapeDtypeStruct(queries.shape, quer...  55.5 us
    unnamed x1, local copies, waits for them, and re-layouts  1.77 us

profile of v2, /device:TPU:1, one launch (start us, length us, event | category | flops | bytes accessed | tf_op | source)
XLA Modules:
  0.0 57.3 jit_solution(9331357743985619275)
XLA Ops:
  0.0 55.5 %shard_map.73 = bf16[32,6144]{1,0:T(8,128)(2,1)} custom-call(bf16[32,6144]{1,0:T(8,128)(2,1)} %q_ref.1, bf16[32,1024]{1,0:T(8,128)(2,1)} %k_ref.1, bf16[32,1024]{1,0:T(8,128)(2,1)} %v_ref.1, s32[64]{0:T(128)} %fold.1, s32[64]{0:T(128)} %noisy.1, s32[64]{0:T(128)} %noise_step.1, f32[64,768]{1,0:T(8,128)} %gate_ref.1), custom_call_target="tpu_custom_call" | custom-call | flops 6442450944 | bytes 1048576 | tf_op jit(solution)/shard_map/pallas_call | solution.py:321
  55.5 1.8 %copy.9 = bf16[32,6144]{1,0:T(8,128)(2,1)} copy(bf16[32,6144]{1,0:T(8,128)(2,1)} %shard_map.73) | data formatting | bytes 786432

commit v3 on v2

--- a/solution.py
+++ b/solution.py
@@ -29,7 +29,7 @@
 
 def kernel(
     q_ref, k_ref, v_ref, fold, noisy, noise_step, gate_ref, out_ref,
-    q_in, k_buf, v_in, vt_buf, qt, m_s, acc, gate_v, ost,
+    q_in, k_loc, v_loc, k_buf, v_in, vt_buf, qt, m_s, acc, gate_v, ost,
     a2a_send, a2a_recv, loc_sem, kv_send, kv_recv, out_send, out_recv,
 ):
     me = lax.axis_index("ctx")
@@ -49,17 +49,13 @@
     peers += [(xb, (1 - xh) * 4 + lax.rem(y + r, 4), lax.rem(y + r, 4), y) for r in range(4)]
     mine = 4 + y
 
-    own_k = pltpu.make_async_copy(
-        k_ref.at[:, pl.ds(pl.multiple_of(h * HD, HD), HD)],
-        k_buf.at[me, pl.ds(pl.multiple_of(mine * ROWS, ROWS), ROWS), :], loc_sem.at[0])
-    own_v = pltpu.make_async_copy(
-        v_ref.at[:, pl.ds(pl.multiple_of(h * HD, HD), HD)],
-        v_in.at[pl.ds(pl.multiple_of(mine * ROWS, ROWS), ROWS), :], loc_sem.at[1])
+    stage_k = pltpu.make_async_copy(k_ref, k_loc, loc_sem.at[0])
+    stage_v = pltpu.make_async_copy(v_ref, v_loc, loc_sem.at[1])
     own_q = pltpu.make_async_copy(
         q_ref.at[:, pl.ds(pl.multiple_of(h * FEAT, FEAT), FEAT)], q_in.at[mine], loc_sem.at[2])
     gates = pltpu.make_async_copy(gate_ref, gate_v, loc_sem.at[3])
-    own_k.start()
-    own_v.start()
+    stage_k.start()
+    stage_v.start()
     own_q.start()
     gates.start()
 
@@ -71,19 +67,21 @@
     vt_buf[:, HD:, :] = jnp.ones((NZ * 4, VROWS - HD, BLOCK), jnp.bfloat16)
     m_s[...] = jnp.full_like(m_s, NEG)
     acc[...] = jnp.zeros_like(acc)
+    stage_k.wait()
+    stage_v.wait()
     pl.semaphore_wait(barrier, NH - 1 + 4)
 
     def k_copy(i, slot, block):
         ctx, head, _, _ = peers[i]
         return pltpu.make_async_remote_copy(
-            k_ref.at[:, pl.ds(pl.multiple_of(head * HD, HD), HD)],
+            k_loc.at[:, pl.ds(pl.multiple_of(head * HD, HD), HD)],
             k_buf.at[block, pl.ds(pl.multiple_of(slot * ROWS, ROWS), ROWS), :],
             a2a_send.at[0, i], a2a_recv.at[0, slot], device_id=(ctx, head), device_id_type=MESH)
 
     def v_copy(i, slot, block):
         ctx, head, _, _ = peers[i]
         return pltpu.make_async_remote_copy(
-            v_ref.at[:, pl.ds(pl.multiple_of(head * HD, HD), HD)],
+            v_loc.at[:, pl.ds(pl.multiple_of(head * HD, HD), HD)],
             v_in.at[pl.ds(pl.multiple_of(slot * ROWS, ROWS), ROWS), :],
             a2a_send.at[1, i], a2a_recv.at[1, slot], device_id=(ctx, head), device_id_type=MESH)
 
@@ -96,6 +94,10 @@
     for copy in (k_copy, v_copy, q_copy):
         for i, peer in enumerate(peers):
             copy(i, peer[3], peer[0]).start()
+    here = pl.ds(pl.multiple_of(h * HD, HD), HD)
+    rows_here = pl.ds(pl.multiple_of(mine * ROWS, ROWS), ROWS)
+    k_buf[me, rows_here, :] = k_loc[:, here]
+    v_in[rows_here, :] = v_loc[:, here]
 
     sent = []
 
@@ -120,37 +122,40 @@
         arrived(half, block)
         send(half, block, *targets, sib)
 
-    own_k.wait()
     for i, peer in enumerate(peers):
         k_copy(i, peer[2], me).wait_recv()
     send(K, me, xb, zp, zm, sib)
-    own_v.wait()
     for i, peer in enumerate(peers):
         v_copy(i, peer[2], me).wait_recv()
     vt_buf[me, :HD, :] = v_in[...].astype(jnp.float32).T.astype(jnp.bfloat16)
     send(V, me, xb, zp, zm, sib)
 
-    def own_k_came(d):
-        come(K, own(-d), zp, xb)
-        come(K, own(d), *((zm,) if d < 3 else ()), xb)
-
-    def own_v_came(d):
-        come(V, own(-d), *((zp,) if d < 3 else ()))
-        come(V, own(d), zm)
-
-    def oth_v_came(d):
-        come(V, oth(-d), *((zp,) if d < 3 else ()))
-        come(V, oth(d), *((zm,) if d < 3 else ()))
-
-    def sibling(d):
-        for x_ in (0, 1):
+    def o_k(*ds):
+        for d in ds:
+            onward = {-1: (zp,), -2: (zp,), -3: (zp,), 1: (zm,), 2: (zm,), 3: (), 4: ()}[d]
+            come(K, own(d), *onward, xb)
+
+    def o_v(*ds):
+        for d in ds:
+            come(V, own(d), *{-1: (zp,), -2: (zp,), -3: (), 1: (zm,), 2: (zm,), 3: (zm,), 4: ()}[d])
+
+    def p_k(*ds):
+        for d in ds:
+            come(K, oth(d))
+
+    def p_v(*ds):
+        for d in ds:
+            come(V, oth(d), *{0: (zp, zm), -1: (zp,), -2: (zp,), -3: (zp,), 1: (zm,), 2: (zm,), 3: (), 4: ()}[d])
+
+    def sibling(x_, *ds):
+        for d in ds:
             for half in (K, V):
                 arrived(half, ctx_of(d, x_, 1 - c))
 
-    come(K, oth(0))
-    own_k_came(1)
-    come(V, oth(0), zp, zm)
-    own_v_came(1)
+    p_k(0)
+    o_k(-1, 1)
+    p_v(0)
+    o_v(-1, 1)
 
     own_q.wait()
     for i, peer in enumerate(peers):
@@ -170,75 +175,82 @@
     gate_rows = [gate_v.at[pl.ds(noise_step[o], 1), :] for o in my_order]
     live = [noisy[o] == 1 for o in my_order]
 
-    def work(zq, slot, done=None):
-        keys = k_buf[pl.ds(zq * 4, 4)].reshape(GROUP, HD)
+    def group(i):
+        away = lax.div(i + 1, 2)
+        col_a = jnp.where(lax.rem(i, 2) == 1, x, 1 - x)
+        col_b = jnp.where((i == 0) | (i == NZ - 1), 1 - col_a, col_a)
+        pairs = []
+        for zq, col in ((lax.rem(z + away, NZ), col_a), (lax.rem(z + NZ - away, NZ), col_b)):
+            pairs.append((zq * 4 + col * 2, 2 - 4 * col))
+        keys = jnp.concatenate([k_buf[pl.ds(b, 2)].reshape(2 * BLOCK, HD) for b, _ in pairs], axis=0)
         keys = jnp.concatenate([keys, keys], axis=1)
-        values = jnp.concatenate([vt_buf[zq * 4 + i] for i in range(4)], axis=1)
-        count = GROUP // SPAN
-        first = 8 * zq
+        values = jnp.concatenate([vt_buf[b + core] for b, _ in pairs for core in range(2)], axis=1)
         orders = []
-        for i in range(4):
-            orders.append(fold[first + 2 * ((i + 2) % 4) + 1 - xh])
-            orders.append(fold[first + 2 * i + xh])
-        slots = (0, 1) if slot is None else (slot,)
-        hide = []
-        for a in slots:
-            order = my_order[a] if isinstance(a, int) else jnp.where(a == 0, my_order[0], my_order[1])
-            hide.append([jnp.where(o <= order, jnp.float32(0), jnp.float32(NEG)) for o in orders])
-        tiles = (TILES // 2) * len(slots)
+        for b, flip in pairs:
+            for core in range(2):
+                orders.append(fold[2 * (b + core + flip) + 1 - xh])
+                orders.append(fold[2 * (b + core) + xh])
+        return keys, values, orders
+
+    def work(numbers, slot, done=None):
+        order = my_order[slot] if isinstance(slot, int) else jnp.where(slot == 0, my_order[0], my_order[1])
+        groups = []
+        for i in numbers:
+            keys, values, orders = group(i)
+            groups.append((keys, values, [jnp.where(o <= order, jnp.float32(0), jnp.float32(NEG)) for o in orders]))
+        half = TILES // 2
+        units = [(g, t) for g in range(len(groups)) for t in range(half)]
 
         def cols(t):
-            if slot is None:
-                return slice(t * TILE, (t + 1) * TILE)
-            return pl.ds(pl.multiple_of((slot * (TILES // 2) + t) * TILE, TILE), TILE)
-
-        def score(t):
-            return jnp.dot(keys, qt[:, cols(t)], preferred_element_type=jnp.float32)
-
-        def soften(t, s):
-            bias = hide[t // (TILES // 2)]
+            return pl.ds(pl.multiple_of((slot * half + t) * TILE, TILE), TILE)
+
+        def score(g, t):
+            return jnp.dot(groups[g][0], qt[:, cols(t)], preferred_element_type=jnp.float32)
+
+        def soften(g, t, s):
+            bias = groups[g][2]
             before = m_s[0:1, cols(t)]
             top = before
-            for i in range(count):
-                top = jnp.maximum(top, jnp.max(s[i * SPAN:(i + 1) * SPAN], axis=0, keepdims=True) + bias[i])
+            for i, b in enumerate(bias):
+                top = jnp.maximum(top, jnp.max(s[i * SPAN:(i + 1) * SPAN], axis=0, keepdims=True) + b)
             probs = [
-                jnp.exp2(s[i * SPAN:(i + 1) * SPAN] - (top - 2 * bias[i])).astype(jnp.bfloat16)
-                for i in range(count)
+                jnp.exp2(s[i * SPAN:(i + 1) * SPAN] - (top - 2 * b)).astype(jnp.bfloat16)
+                for i, b in enumerate(bias)
             ]
             m_s[0:1, cols(t)] = top
             return jnp.concatenate(probs, axis=0), jnp.exp2(before - top)
 
-        def add(t, probs, alpha):
-            total = acc[:, cols(t)] * alpha + jnp.dot(values, probs, preferred_element_type=jnp.float32)
-            if done is None:
+        def add(g, t, probs, alpha):
+            total = acc[:, cols(t)] * alpha + jnp.dot(groups[g][1], probs, preferred_element_type=jnp.float32)
+            if done is None or g < len(groups) - 1:
                 acc[:, cols(t)] = total
             else:
-                done(t, total)
-
-        s = score(0)
+                done(slot * half + t, total)
+
+        s = score(*units[0])
         held = None
-        for t in range(tiles):
-            following = score(t + 1) if t + 1 < tiles else None
+        for n, unit in enumerate(units):
+            following = score(*units[n + 1]) if n + 1 < len(units) else None
             if held is not None:
-                add(t - 1, *held)
-            held = soften(t, s)
+                add(*units[n - 1], *held)
+            held = soften(*unit, s)
             s = following
-        add(tiles - 1, *held)
+        add(*units[-1], *held)
 
     events = {
-        0: lambda: sibling(0),
-        1: lambda: (own_k_came(2), come(K, oth(1))),
-        2: lambda: (oth_v_came(1), come(K, oth(-1)), sibling(1), sibling(-1)),
-        3: lambda: (own_v_came(2), come(K, oth(2))),
-        4: lambda: (own_k_came(3), come(K, oth(-2))),
-        5: lambda: oth_v_came(2),
-        6: lambda: (sibling(2), sibling(-2)),
-        7: lambda: (own_v_came(3), come(K, oth(3))),
-        8: lambda: (come(K, own(4), xb), come(K, oth(-3))),
-        9: lambda: oth_v_came(3),
-        10: lambda: (come(V, own(4), xb), sibling(3), sibling(-3)),
-        12: lambda: come(K, oth(4)),
-        13: lambda: come(V, oth(4)),
+        0: lambda: (sibling(x, 0), sibling(1 - x, 0)),
+        1: lambda: (o_k(-2, 2), p_k(-1)),
+        2: lambda: (p_k(1), p_v(-1, 1), sibling(x, -1, 1)),
+        3: lambda: o_v(-2, 2),
+        4: lambda: (p_k(-2), sibling(1 - x, -1, 1)),
+        5: lambda: (o_k(-3, 3), p_k(2)),
+        6: lambda: (p_v(-2, 2), sibling(x, -2, 2)),
+        7: lambda: o_v(-3, 3),
+        8: lambda: sibling(1 - x, -2, 2),
+        9: lambda: (o_k(4), p_k(-3)),
+        10: lambda: (p_v(-3, 3), p_k(3), sibling(x, -3, 3)),
+        11: lambda: o_v(4),
+        12: lambda: (p_k(4), sibling(1 - x, -3, 3)),
     }
 
     def step(u, carry):
@@ -246,14 +258,13 @@
             @pl.when(u == at)
             def _():
                 todo()
-        i = lax.div(u, 2)
-        near = lax.div(i + 1, 2)
-        d = jnp.where(lax.rem(i, 2) == 1, near, NZ - near)
-        work(lax.rem(z + d, NZ), lax.rem(u, 2))
+        work([lax.div(u, 2)], lax.rem(u, 2))
         return carry
 
-    lax.fori_loop(0, 2 * (NZ - 1), step, 0)
-    sibling(4)
+    lax.fori_loop(0, 2 * NZ - 3, step, 0)
+    p_v(4)
+    sibling(x, 4)
+    sibling(1 - x, 4)
 
     results = []
 
@@ -293,7 +304,8 @@
             result_copy(t, part, len(results)).start()
             results.append((t, part))
 
-    work(lax.rem(z + 4, NZ), None, done)
+    work([NZ - 1], 0, done)
+    work([NZ - 2, NZ - 1], 1, done)
 
     for jp in range(3):
         own_result(3 + jp).wait()
@@ -325,6 +337,8 @@
         out_specs=hbm,
         scratch_shapes=[
             pltpu.VMEM((NH, ROWS, FEAT), jnp.bfloat16),
+            pltpu.VMEM(keys.shape, jnp.bfloat16),
+            pltpu.VMEM(values.shape, jnp.bfloat16),
             pltpu.VMEM((blocks, BLOCK, HD), jnp.bfloat16),
             pltpu.VMEM((BLOCK, HD), jnp.bfloat16),
             pltpu.VMEM((blocks, VROWS, BLOCK), jnp.bfloat16),

time: 57.4 us -> 55.8 us (0.972)
  Pallas kernels: 55.5 us -> 53.9 us
    pallas_call x1, Pallas kernels: 55.5 us -> 53.9 us  [local(): pl.pallas_call(kernel, out_shape=jax.ShapeDtypeStruct(queries.shape, quer...]
where the time goes in v3:
time: 55.8 us; the launch traced here: 55.6 us
  Pallas kernels  53.9 us (97%)
  local copies, waits for them, and re-layouts  1.77 us (3%)
    pallas_call x1, Pallas kernels, local(): pl.pallas_call(kernel, out_shape=jax.ShapeDtypeStruct(queries.shape, quer...  53.9 us
    unnamed x1, local copies, waits for them, and re-layouts  1.77 us

profile of v3, /device:TPU:1, one launch (start us, length us, event | category | flops | bytes accessed | tf_op | source)
XLA Modules:
  0.0 55.6 jit_solution(433965754836896383)
XLA Ops:
  0.0 53.9 %shard_map.73 = bf16[32,6144]{1,0:T(8,128)(2,1)} custom-call(bf16[32,6144]{1,0:T(8,128)(2,1)} %q_ref.1, bf16[32,1024]{1,0:T(8,128)(2,1)} %k_ref.1, bf16[32,1024]{1,0:T(8,128)(2,1)} %v_ref.1, s32[64]{0:T(128)} %fold.1, s32[64]{0:T(128)} %noisy.1, s32[64]{0:T(128)} %noise_step.1, f32[64,768]{1,0:T(8,128)} %gate_ref.1), custom_call_target="tpu_custom_call" | custom-call | flops 6442450944 | bytes 1048576 | tf_op jit(solution)/shard_map/pallas_call | solution.py:333
  53.9 1.8 %copy.9 = bf16[32,6144]{1,0:T(8,128)(2,1)} copy(bf16[32,6144]{1,0:T(8,128)(2,1)} %shard_map.73) | data formatting | bytes 786432

commit v4 on v3

--- a/solution.py
+++ b/solution.py
@@ -100,62 +100,50 @@
     v_in[rows_here, :] = v_loc[:, here]
 
     sent = []
-
-    def block_copy(half, block, target, send):
+    targets = dict(zp=zp, zm=zm, xb=xb, sib=sib)
+    links = list(targets)
+
+    def block_of(column, d, core):
+        return ctx_of(d, x if column == 0 else 1 - x, core)
+
+    def block_copy(half, block, link, column, d):
         ref = k_buf.at[block] if half == K else vt_buf.at[block, pl.ds(0, HD), :]
         return pltpu.make_async_remote_copy(
-            ref, ref, kv_send.at[send], kv_recv.at[half, block],
-            device_id=(target, h), device_id_type=MESH)
-
-    def send(half, block, *targets):
-        for target in targets:
-            block_copy(half, block, target, len(sent)).start()
-            sent.append((half, block, target))
-
-    def arrived(half, block):
-        block_copy(half, block, sib, 0).wait_recv()
-
-    own = lambda d: ctx_of(d, x, c)
-    oth = lambda d: ctx_of(d, 1 - x, c)
-
-    def come(half, block, *targets):
-        arrived(half, block)
-        send(half, block, *targets, sib)
+            ref, ref, kv_send.at[links.index(link), half, column * NZ + lax.rem(d + NZ, NZ)],
+            kv_recv.at[half, block], device_id=(targets[link], h), device_id_type=MESH)
+
+    def send(half, column, d, *onto, ds=None):
+        for link in onto:
+            block_copy(half, block_of(column, d, c), link, column, d).start()
+            for value in (d,) if ds is None else ds:
+                sent.append((half, column, value, link))
+
+    def arrived(half, column, d, core=c):
+        block_copy(half, block_of(column, d, core), "sib", column, d).wait_recv()
+
+    def come(half, column, d, *onto, ds=None):
+        arrived(half, column, d)
+        send(half, column, d, *onto, "sib", ds=ds)
+
+    def sibling(column, *steps):
+        for d in steps:
+            for half in (K, V):
+                arrived(half, column, d, 1 - c)
 
     for i, peer in enumerate(peers):
         k_copy(i, peer[2], me).wait_recv()
-    send(K, me, xb, zp, zm, sib)
+    send(K, 0, 0, *links)
     for i, peer in enumerate(peers):
         v_copy(i, peer[2], me).wait_recv()
     vt_buf[me, :HD, :] = v_in[...].astype(jnp.float32).T.astype(jnp.bfloat16)
-    send(V, me, xb, zp, zm, sib)
-
-    def o_k(*ds):
-        for d in ds:
-            onward = {-1: (zp,), -2: (zp,), -3: (zp,), 1: (zm,), 2: (zm,), 3: (), 4: ()}[d]
-            come(K, own(d), *onward, xb)
-
-    def o_v(*ds):
-        for d in ds:
-            come(V, own(d), *{-1: (zp,), -2: (zp,), -3: (), 1: (zm,), 2: (zm,), 3: (zm,), 4: ()}[d])
-
-    def p_k(*ds):
-        for d in ds:
-            come(K, oth(d))
-
-    def p_v(*ds):
-        for d in ds:
-            come(V, oth(d), *{0: (zp, zm), -1: (zp,), -2: (zp,), -3: (zp,), 1: (zm,), 2: (zm,), 3: (), 4: ()}[d])
-
-    def sibling(x_, *ds):
-        for d in ds:
-            for half in (K, V):
-                arrived(half, ctx_of(d, x_, 1 - c))
-
-    p_k(0)
-    o_k(-1, 1)
-    p_v(0)
-    o_v(-1, 1)
+    send(V, 0, 0, *links)
+
+    come(K, 1, 0)
+    come(K, 0, -1, "zp", "xb")
+    come(K, 0, 1, "zm", "xb")
+    come(V, 1, 0, "zp", "zm")
+    come(V, 0, -1, "zp")
+    come(V, 0, 1, "zm")
 
     own_q.wait()
     for i, peer in enumerate(peers):
@@ -237,34 +225,76 @@
             s = following
         add(*units[-1], *held)
 
-    events = {
-        0: lambda: (sibling(x, 0), sibling(1 - x, 0)),
-        1: lambda: (o_k(-2, 2), p_k(-1)),
-        2: lambda: (p_k(1), p_v(-1, 1), sibling(x, -1, 1)),
-        3: lambda: o_v(-2, 2),
-        4: lambda: (p_k(-2), sibling(1 - x, -1, 1)),
-        5: lambda: (o_k(-3, 3), p_k(2)),
-        6: lambda: (p_v(-2, 2), sibling(x, -2, 2)),
-        7: lambda: o_v(-3, 3),
-        8: lambda: sibling(1 - x, -2, 2),
-        9: lambda: (o_k(4), p_k(-3)),
-        10: lambda: (p_v(-3, 3), p_k(3), sibling(x, -3, 3)),
-        11: lambda: o_v(4),
-        12: lambda: (p_k(4), sibling(1 - x, -3, 3)),
-    }
-
-    def step(u, carry):
-        for at, todo in events.items():
-            @pl.when(u == at)
-            def _():
-                todo()
-        work([lax.div(u, 2)], lax.rem(u, 2))
+    def round_of(d, carry):
+        @pl.when(d == 1)
+        def _():
+            sibling(0, 0)
+            sibling(1, 0)
+
+        @pl.when(d > 1)
+        def _():
+            sibling(1, 1 - d, d - 1)
+
+        work([2 * d - 2], 0)
+
+        @pl.when(d < 3)
+        def _():
+            come(K, 0, -d - 1, "zp", "xb", ds=(-2, -3))
+
+        arrived(K, 0, d + 1)
+
+        @pl.when(d == 1)
+        def _():
+            send(K, 0, d + 1, "zm", ds=(2,))
+
+        send(K, 0, d + 1, "xb", "sib", ds=(2, 3, 4))
+        come(K, 1, -d, ds=(-1, -2, -3))
+        work([2 * d - 2], 1)
+
+        come(K, 1, d, ds=(1, 2, 3))
+        come(V, 1, -d, "zp", ds=(-1, -2, -3))
+        arrived(V, 1, d)
+
+        @pl.when(d < 3)
+        def _():
+            send(V, 1, d, "zm", ds=(1, 2))
+
+        send(V, 1, d, "sib", ds=(1, 2, 3))
+        sibling(0, -d, d)
+        work([2 * d - 1], 0)
+
+        @pl.when(d < 3)
+        def _():
+            arrived(V, 0, -d - 1)
+
+        @pl.when(d == 1)
+        def _():
+            send(V, 0, -d - 1, "zp", ds=(-2,))
+
+        @pl.when(d < 3)
+        def _():
+            send(V, 0, -d - 1, "sib", ds=(-2, -3))
+
+        arrived(V, 0, d + 1)
+
+        @pl.when(d < 3)
+        def _():
+            send(V, 0, d + 1, "zm", ds=(2, 3))
+
+        send(V, 0, d + 1, "sib", ds=(2, 3, 4))
+
+        @pl.when(d == 3)
+        def _():
+            sibling(1, -d, d)
+
+        work([jnp.where(d == 3, NZ - 2, 2 * d - 1)], jnp.where(d == 3, 0, 1))
         return carry
 
-    lax.fori_loop(0, 2 * NZ - 3, step, 0)
-    p_v(4)
-    sibling(x, 4)
-    sibling(1 - x, 4)
+    lax.fori_loop(1, 4, round_of, 0)
+    come(K, 1, 4)
+    come(V, 1, 4)
+    sibling(0, 4)
+    sibling(1, 4)
 
     results = []
 
@@ -305,7 +335,7 @@
             results.append((t, part))
 
     work([NZ - 1], 0, done)
-    work([NZ - 2, NZ - 1], 1, done)
+    work([NZ - 3, NZ - 2, NZ - 1], 1, done)
 
     for jp in range(3):
         own_result(3 + jp).wait()
@@ -314,8 +344,8 @@
     for i, peer in enumerate(peers):
         for copy in (k_copy, v_copy, q_copy):
             copy(i, peer[3], peer[0]).wait_send()
-    for i, (half, block, target) in enumerate(sent):
-        block_copy(half, me, sib, i).wait_send()
+    for half, column, d, link in sent:
+        block_copy(half, me, link, column, d).wait_send()
     for ctx, head, _, _ in peers:
         for jp in range(3):
             pltpu.make_async_remote_copy(
@@ -350,7 +380,7 @@
             pltpu.SemaphoreType.DMA((3, NH)),
             pltpu.SemaphoreType.DMA((3, NH)),
             pltpu.SemaphoreType.DMA((8,)),
-            pltpu.SemaphoreType.DMA((64,)),
+            pltpu.SemaphoreType.DMA((4, 2, 2 * NZ)),
             pltpu.SemaphoreType.DMA((2, blocks)),
             pltpu.SemaphoreType.DMA((24,)),
             pltpu.SemaphoreType.DMA((NH, 3)),

time: 55.8 us -> 53.5 us (0.959)
  Pallas kernels: 53.9 us -> 51.6 us
    pallas_call x1, Pallas kernels: 53.9 us -> 51.6 us  [local(): pl.pallas_call(kernel, out_shape=jax.ShapeDtypeStruct(queries.shape, quer...]
where the time goes in v4:
time: 53.5 us; the launch traced here: 53.4 us
  Pallas kernels  51.6 us (96%)
  local copies, waits for them, and re-layouts  1.77 us (3%)
    pallas_call x1, Pallas kernels, local(): pl.pallas_call(kernel, out_shape=jax.ShapeDtypeStruct(queries.shape, quer...  51.6 us
    unnamed x1, local copies, waits for them, and re-layouts  1.77 us

profile of v4, /device:TPU:1, one launch (start us, length us, event | category | flops | bytes accessed | tf_op | source)
XLA Modules:
  0.0 53.4 jit_solution(17960773109108096357)
XLA Ops:
  0.0 51.6 %shard_map.73 = bf16[32,6144]{1,0:T(8,128)(2,1)} custom-call(bf16[32,6144]{1,0:T(8,128)(2,1)} %q_ref.1, bf16[32,1024]{1,0:T(8,128)(2,1)} %k_ref.1, bf16[32,1024]{1,0:T(8,128)(2,1)} %v_ref.1, s32[64]{0:T(128)} %fold.1, s32[64]{0:T(128)} %noisy.1, s32[64]{0:T(128)} %noise_step.1, f32[64,768]{1,0:T(8,128)} %gate_ref.1), custom_call_target="tpu_custom_call" | custom-call | flops 6442450944 | bytes 1048576 | tf_op jit(solution)/shard_map/pallas_call | solution.py:363
  51.6 1.8 %copy.9 = bf16[32,6144]{1,0:T(8,128)(2,1)} copy(bf16[32,6144]{1,0:T(8,128)(2,1)} %shard_map.73) | data formatting | bytes 786432

commit v5 on v4

--- a/solution.py
+++ b/solution.py
@@ -180,24 +180,30 @@
                 orders.append(fold[2 * (b + core) + xh])
         return keys, values, orders
 
-    def work(numbers, slot, done=None):
-        order = my_order[slot] if isinstance(slot, int) else jnp.where(slot == 0, my_order[0], my_order[1])
-        groups = []
-        for i in numbers:
-            keys, values, orders = group(i)
-            groups.append((keys, values, [jnp.where(o <= order, jnp.float32(0), jnp.float32(NEG)) for o in orders]))
+    def work(*parts):
         half = TILES // 2
-        units = [(g, t) for g in range(len(groups)) for t in range(half)]
-
-        def cols(t):
-            return pl.ds(pl.multiple_of((slot * half + t) * TILE, TILE), TILE)
-
-        def score(g, t):
-            return jnp.dot(groups[g][0], qt[:, cols(t)], preferred_element_type=jnp.float32)
-
-        def soften(g, t, s):
-            bias = groups[g][2]
-            before = m_s[0:1, cols(t)]
+        units = [(p, t) for p in range(len(parts)) for t in range(half)]
+        groups = {}
+
+        def enter(p):
+            before, number, slot, _ = parts[p]
+            if before is not None:
+                before()
+            order = my_order[slot] if isinstance(slot, int) else jnp.where(slot == 0, my_order[0], my_order[1])
+            keys, values, orders = group(number)
+            groups[p] = keys, values, [jnp.where(o <= order, jnp.float32(0), jnp.float32(NEG)) for o in orders]
+
+        def cols(p, t):
+            return pl.ds(pl.multiple_of((parts[p][2] * half + t) * TILE, TILE), TILE)
+
+        def score(p, t):
+            if p not in groups:
+                enter(p)
+            return jnp.dot(groups[p][0], qt[:, cols(p, t)], preferred_element_type=jnp.float32)
+
+        def soften(p, t, s):
+            bias = groups[p][2]
+            before = m_s[0:1, cols(p, t)]
             top = before
             for i, b in enumerate(bias):
                 top = jnp.maximum(top, jnp.max(s[i * SPAN:(i + 1) * SPAN], axis=0, keepdims=True) + b)
@@ -205,15 +211,15 @@
                 jnp.exp2(s[i * SPAN:(i + 1) * SPAN] - (top - 2 * b)).astype(jnp.bfloat16)
                 for i, b in enumerate(bias)
             ]
-            m_s[0:1, cols(t)] = top
+            m_s[0:1, cols(p, t)] = top
             return jnp.concatenate(probs, axis=0), jnp.exp2(before - top)
 
-        def add(g, t, probs, alpha):
-            total = acc[:, cols(t)] * alpha + jnp.dot(groups[g][1], probs, preferred_element_type=jnp.float32)
-            if done is None or g < len(groups) - 1:
-                acc[:, cols(t)] = total
+        def add(p, t, probs, alpha):
+            total = acc[:, cols(p, t)] * alpha + jnp.dot(groups[p][1], probs, preferred_element_type=jnp.float32)
+            if parts[p][3] is None:
+                acc[:, cols(p, t)] = total
             else:
-                done(slot * half + t, total)
+                parts[p][3](parts[p][2] * half + t, total)
 
         s = score(*units[0])
         held = None
@@ -226,68 +232,73 @@
         add(*units[-1], *held)
 
     def round_of(d, carry):
-        @pl.when(d == 1)
-        def _():
-            sibling(0, 0)
-            sibling(1, 0)
-
-        @pl.when(d > 1)
-        def _():
-            sibling(1, 1 - d, d - 1)
-
-        work([2 * d - 2], 0)
-
-        @pl.when(d < 3)
-        def _():
-            come(K, 0, -d - 1, "zp", "xb", ds=(-2, -3))
-
-        arrived(K, 0, d + 1)
-
-        @pl.when(d == 1)
-        def _():
-            send(K, 0, d + 1, "zm", ds=(2,))
-
-        send(K, 0, d + 1, "xb", "sib", ds=(2, 3, 4))
-        come(K, 1, -d, ds=(-1, -2, -3))
-        work([2 * d - 2], 1)
-
-        come(K, 1, d, ds=(1, 2, 3))
-        come(V, 1, -d, "zp", ds=(-1, -2, -3))
-        arrived(V, 1, d)
-
-        @pl.when(d < 3)
-        def _():
-            send(V, 1, d, "zm", ds=(1, 2))
-
-        send(V, 1, d, "sib", ds=(1, 2, 3))
-        sibling(0, -d, d)
-        work([2 * d - 1], 0)
-
-        @pl.when(d < 3)
-        def _():
-            arrived(V, 0, -d - 1)
-
-        @pl.when(d == 1)
-        def _():
-            send(V, 0, -d - 1, "zp", ds=(-2,))
-
-        @pl.when(d < 3)
-        def _():
-            send(V, 0, -d - 1, "sib", ds=(-2, -3))
-
-        arrived(V, 0, d + 1)
-
-        @pl.when(d < 3)
-        def _():
-            send(V, 0, d + 1, "zm", ds=(2, 3))
-
-        send(V, 0, d + 1, "sib", ds=(2, 3, 4))
-
-        @pl.when(d == 3)
-        def _():
-            sibling(1, -d, d)
-
-        work([jnp.where(d == 3, NZ - 2, 2 * d - 1)], jnp.where(d == 3, 0, 1))
+        def first():
+            @pl.when(d == 1)
+            def _():
+                sibling(0, 0)
+                sibling(1, 0)
+
+            @pl.when(d > 1)
+            def _():
+                sibling(1, 1 - d, d - 1)
+
+        def second():
+            @pl.when(d < 3)
+            def _():
+                come(K, 0, -d - 1, "zp", "xb", ds=(-2, -3))
+
+            arrived(K, 0, d + 1)
+
+            @pl.when(d == 1)
+            def _():
+                send(K, 0, d + 1, "zm", ds=(2,))
+
+            send(K, 0, d + 1, "xb", "sib", ds=(2, 3, 4))
+            come(K, 1, -d, ds=(-1, -2, -3))
+
+        def third():
+            come(K, 1, d, ds=(1, 2, 3))
+            come(V, 1, -d, "zp", ds=(-1, -2, -3))
+            arrived(V, 1, d)
+
+            @pl.when(d < 3)
+            def _():
+                send(V, 1, d, "zm", ds=(1, 2))
+
+            send(V, 1, d, "sib", ds=(1, 2, 3))
+            sibling(0, -d, d)
+
+        def fourth():
+            @pl.when(d < 3)
+            def _():
+                arrived(V, 0, -d - 1)
+
+            @pl.when(d == 1)
+            def _():
+                send(V, 0, -d - 1, "zp", ds=(-2,))
+
+            @pl.when(d < 3)
+            def _():
+                send(V, 0, -d - 1, "sib", ds=(-2, -3))
+
+            arrived(V, 0, d + 1)
+
+            @pl.when(d < 3)
+            def _():
+                send(V, 0, d + 1, "zm", ds=(2, 3))
+
+            send(V, 0, d + 1, "sib", ds=(2, 3, 4))
+
+            @pl.when(d == 3)
+            def _():
+                sibling(1, -d, d)
+
+        work(
+            (first, 2 * d - 2, 0, None),
+            (second, 2 * d - 2, 1, None),
+            (third, 2 * d - 1, 0, None),
+            (fourth, jnp.where(d == 3, NZ - 2, 2 * d - 1), jnp.where(d == 3, 0, 1), None),
+        )
         return carry
 
     lax.fori_loop(1, 4, round_of, 0)
@@ -334,8 +345,7 @@
             result_copy(t, part, len(results)).start()
             results.append((t, part))
 
-    work([NZ - 1], 0, done)
-    work([NZ - 3, NZ - 2, NZ - 1], 1, done)
+    work((None, NZ - 1, 0, done), *((None, NZ - 3 + i, 1, done if i == 2 else None) for i in range(3)))
 
     for jp in range(3):
         own_result(3 + jp).wait()

time: 53.5 us -> 52.8 us (0.987)
  Pallas kernels: 51.6 us -> 50.9 us
    pallas_call x1, Pallas kernels: 51.6 us -> 50.9 us  [local(): pl.pallas_call(kernel, out_shape=jax.ShapeDtypeStruct(queries.shape, quer...]
where the time goes in v5:
time: 52.8 us; the launch traced here: 52.7 us
  Pallas kernels  50.9 us (96%)
  local copies, waits for them, and re-layouts  1.77 us (3%)
    pallas_call x1, Pallas kernels, local(): pl.pallas_call(kernel, out_shape=jax.ShapeDtypeStruct(queries.shape, quer...  50.9 us
    unnamed x1, local copies, waits for them, and re-layouts  1.77 us

profile of v5, /device:TPU:1, one launch (start us, length us, event | category | flops | bytes accessed | tf_op | source)
XLA Modules:
  0.0 52.7 jit_solution(2187068408457147285)
XLA Ops:
  0.0 50.9 %shard_map.73 = bf16[32,6144]{1,0:T(8,128)(2,1)} custom-call(bf16[32,6144]{1,0:T(8,128)(2,1)} %q_ref.1, bf16[32,1024]{1,0:T(8,128)(2,1)} %k_ref.1, bf16[32,1024]{1,0:T(8,128)(2,1)} %v_ref.1, s32[64]{0:T(128)} %fold.1, s32[64]{0:T(128)} %noisy.1, s32[64]{0:T(128)} %noise_step.1, f32[64,768]{1,0:T(8,128)} %gate_ref.1), custom_call_target="tpu_custom_call" | custom-call | flops 6442450944 | bytes 1048576 | tf_op jit(solution)/shard_map/pallas_call | solution.py:373
  50.9 1.8 %copy.9 = bf16[32,6144]{1,0:T(8,128)(2,1)} copy(bf16[32,6144]{1,0:T(8,128)(2,1)} %shard_map.73) | data formatting | bytes 786432

commit v6 on v5

--- a/solution.py
+++ b/solution.py
@@ -45,8 +45,8 @@
 
     zp, zm = ctx_of(1, x, c), ctx_of(-1, x, c)
     xb, sib = ctx_of(0, 1 - x, c), ctx_of(0, x, 1 - c)
-    peers = [(me, xh * 4 + lax.rem(y + r, 4), 4 + lax.rem(y + r, 4), 4 + y) for r in range(1, 4)]
-    peers += [(xb, (1 - xh) * 4 + lax.rem(y + r, 4), lax.rem(y + r, 4), y) for r in range(4)]
+    peers = [(me, xh * 4 + lax.rem(y + r, 4), 4 + lax.rem(y + r, 4), 4 + y) for r in (2, 1, 3)]
+    peers += [(xb, (1 - xh) * 4 + lax.rem(y + r, 4), lax.rem(y + r, 4), y) for r in (2, 1, 3, 0)]
     mine = 4 + y
 
     stage_k = pltpu.make_async_copy(k_ref, k_loc, loc_sem.at[0])
@@ -302,10 +302,12 @@
         return carry
 
     lax.fori_loop(1, 4, round_of, 0)
-    come(K, 1, 4)
-    come(V, 1, 4)
-    sibling(0, 4)
-    sibling(1, 4)
+
+    def opposite():
+        come(K, 1, 4)
+        come(V, 1, 4)
+        sibling(0, 4)
+        sibling(1, 4)
 
     results = []
 
@@ -345,7 +347,12 @@
             result_copy(t, part, len(results)).start()
             results.append((t, part))
 
-    work((None, NZ - 1, 0, done), *((None, NZ - 3 + i, 1, done if i == 2 else None) for i in range(3)))
+    work(
+        (None, NZ - 3, 1, None),
+        (opposite, NZ - 1, 0, done),
+        (None, NZ - 2, 1, None),
+        (None, NZ - 1, 1, done),
+    )
 
     for jp in range(3):
         own_result(3 + jp).wait()

time: 52.8 us -> 52.9 us (level)
  no operation moved by 1% of the time
where the time goes in v6:
time: 52.9 us; the launch traced here: 52.8 us
  Pallas kernels  51 us (96%)
  local copies, waits for them, and re-layouts  1.77 us (3%)
    pallas_call x1, Pallas kernels, local(): pl.pallas_call(kernel, out_shape=jax.ShapeDtypeStruct(queries.shape, quer...  51 us
    unnamed x1, local copies, waits for them, and re-layouts  1.77 us

profile of v6, /device:TPU:1, one launch (start us, length us, event | category | flops | bytes accessed | tf_op | source)
XLA Modules:
  0.0 52.8 jit_solution(4135713764281115252)
XLA Ops:
  0.0 51.0 %shard_map.73 = bf16[32,6144]{1,0:T(8,128)(2,1)} custom-call(bf16[32,6144]{1,0:T(8,128)(2,1)} %q_ref.1, bf16[32,1024]{1,0:T(8,128)(2,1)} %k_ref.1, bf16[32,1024]{1,0:T(8,128)(2,1)} %v_ref.1, s32[64]{0:T(128)} %fold.1, s32[64]{0:T(128)} %noisy.1, s32[64]{0:T(128)} %noise_step.1, f32[64,768]{1,0:T(8,128)} %gate_ref.1), custom_call_target="tpu_custom_call" | custom-call | flops 6442450944 | bytes 1048576 | tf_op jit(solution)/shard_map/pallas_call | solution.py:380
  51.0 1.8 %copy.9 = bf16[32,6144]{1,0:T(8,128)(2,1)} copy(bf16[32,6144]{1,0:T(8,128)(2,1)} %shard_map.73) | data formatting | bytes 786432

commit v7 on v6

--- a/solution.py
+++ b/solution.py
@@ -28,7 +28,7 @@
 
 
 def kernel(
-    q_ref, k_ref, v_ref, fold, noisy, noise_step, gate_ref, out_ref,
+    q_ref, k_ref, v_ref, fold, noisy, noise_step, gate_ref, out_ref, live_ref,
     q_in, k_loc, v_loc, k_buf, v_in, vt_buf, qt, m_s, acc, gate_v, ost,
     a2a_send, a2a_recv, loc_sem, kv_send, kv_recv, out_send, out_recv,
 ):
@@ -161,7 +161,7 @@
 
     my_order = [fold[2 * xb + 1 - xh], fold[2 * me + xh]]
     gate_rows = [gate_v.at[pl.ds(noise_step[o], 1), :] for o in my_order]
-    live = [noisy[o] == 1 for o in my_order]
+    live_ref[...] = jnp.full(live_ref.shape, jnp.where(noisy[my_order[1]] == 1, jnp.float32(1), jnp.float32(0)))
 
     def group(i):
         away = lax.div(i + 1, 2)
@@ -337,7 +337,6 @@
             j = 2 * jp + jj
             rows = scaled[:, jj * HD:(jj + 1) * HD].T
             rows = rows * gate_rows[slot][:, j * HD:(j + 1) * HD]
-            rows = jnp.where(live[slot], rows, jnp.float32(0))
             ost[t, :, jj * HD:(jj + 1) * HD] = rows.astype(jnp.bfloat16)
         for r in range(4):
             part = lax.rem(y + r, 4)
@@ -377,11 +376,14 @@
     smem = pl.BlockSpec(memory_space=pltpu.SMEM)
     width = 2 * SPAN * RATIO
     blocks = NZ * 4
-    return pl.pallas_call(
+    gated, live = pl.pallas_call(
         kernel,
-        out_shape=jax.ShapeDtypeStruct(queries.shape, queries.dtype),
+        out_shape=(
+            jax.ShapeDtypeStruct(queries.shape, queries.dtype),
+            jax.ShapeDtypeStruct((8, queries.shape[1]), jnp.float32),
+        ),
         in_specs=[hbm, hbm, hbm, smem, smem, smem, hbm],
-        out_specs=hbm,
+        out_specs=(hbm, pl.BlockSpec(memory_space=pltpu.VMEM)),
         scratch_shapes=[
             pltpu.VMEM((NH, ROWS, FEAT), jnp.bfloat16),
             pltpu.VMEM(keys.shape, jnp.bfloat16),
@@ -409,6 +411,7 @@
             flops=2 * 2 * width * 8192 * HD, bytes_accessed=2**20, transcendentals=width * 8192
         ),
     )(queries, keys, values, fold_map, noisy, noise_step, gate_table)
+    return jnp.where(live[:1] > 0, gated, jnp.zeros_like(gated))
 
 
 def solution(mesh):

time: 52.9 us -> 54.7 us (1.034)
  other arithmetic: 0 us -> 2.79 us
  local copies, waits for them, and re-layouts: 1.77 us -> 0 us
  Pallas kernels: 51 us -> 51.7 us
    select_n x0 -> x1, other arithmetic: none -> 1.79 us  [local(): return jnp.where(live[:1] > 0, gated, jnp.zeros_like(gated))]
    unnamed x1 -> x0, local copies, waits for them, and re-layouts: 1.77 us -> none
    gt x0 -> x1, other arithmetic: none -> 1 us  [local(): return jnp.where(live[:1] > 0, gated, jnp.zeros_like(gated))]
    pallas_call x1, Pallas kernels: 51 us -> 51.7 us  [local(): pl.pallas_call(kernel, out_shape=(jax.ShapeDtypeStruct(queries.shape, que...]
where the time goes in v7:
time: 54.7 us; the launch traced here: 54.5 us
  Pallas kernels  51.7 us (95%)
  other arithmetic  2.79 us (5%)
    pallas_call x1, Pallas kernels, local(): pl.pallas_call(kernel, out_shape=(jax.ShapeDtypeStruct(queries.shape, que...  51.7 us
    select_n x1, other arithmetic, local(): return jnp.where(live[:1] > 0, gated, jnp.zeros_like(gated))  1.79 us

profile of v7, /device:TPU:1, one launch (start us, length us, event | category | flops | bytes accessed | tf_op | source)
XLA Modules:
  0.0 54.5 jit_solution(18367492163156291155)
XLA Ops:
  0.0 51.7 %shard_map.73 = (bf16[32,6144]{1,0:T(8,128)(2,1)}, f32[8,6144]{1,0:T(8,128)}) custom-call(bf16[32,6144]{1,0:T(8,128)(2,1)} %q_ref.1, bf16[32,1024]{1,0:T(8,128)(2,1)} %k_ref.1, bf16[32,1024]{1,0:T(8,128)(2,1)} %v_ref.1, s32[64]{0:T(128)} %fold.1, s32[64]{0:T(128)} %noisy.1, s32[64]{0:T(128)} %noise_step.1, f32[64,768]{1,0:T(8,128)} %gate_ref.1), custom_call_target="tpu_custom_call" | custom-call | flops 6442450944 | bytes 1048576 | tf_op jit(solution)/shard_map/pallas_call | solution.py:379
  51.7 1.0 %compare_reduce_fusion = pred[6144]{0:T(1024)(128)(4,1)S(1)} fusion(f32[8,6144]{1,0:T(8,128)} %get-tuple-element.7), kind=kLoop, calls=%fused_computation.1 | loop fusion | flops 6144 | bytes 30720 | tf_op jit(solution)/shard_map/gt | solution.py:414
  52.7 1.8 %broadcast_select_fusion = bf16[32,6144]{1,0:T(8,128)(2,1)} fusion(bf16[32,6144]{1,0:T(8,128)(2,1)} %get-tuple-element.8, pred[6144]{0:T(1024)(128)(4,1)S(1)} %compare_reduce_fusion), kind=kLoop, calls=%fused_computation | loop fusion | flops 196608 | bytes 792576 | tf_op jit(solution)/shard_map/jit(_where)/select_n | solution.py:414
